TPU v7x, 256 devices: a whole 4x4x8 slice. The times are simulated.
256 devices in a mesh: dp: 64 (over x, y, z_lo), mp: 4 (over z_hi, core).
Axes of the slice: x: 4, y: 4, z: 8 (z_hi: 2, z_lo: 4; z = z_hi * 4 + z_lo), core: 2. Of those that a mesh axis runs over, the one named last changes fastest.
Arguments:
- grad: bfloat16 [16384, 8192], P('dp', 'mp'), may hold values from -6 to 6
- right_basis: bfloat16 [8, 1024, 1024], P('mp', 'dp'), may hold values from -0.1875 to 0.1875
- left_basis: bfloat16 [16, 1024, 1024], P('mp', 'dp'), may hold values from -0.1875 to 0.1875
- first_moment: float32 [16384, 8192], P('mp', 'dp'), may hold values from -6 to 6
- second_moment: float32 [16384, 8192], P('mp', 'dp'), may hold values from 0.1 to 10
Outputs:
- update: float32 [16384, 8192], P('dp', 'mp')
- first_new: float32 [16384, 8192], P('mp', 'dp')
- second_new: float32 [16384, 8192], P('mp', 'dp')
All inputs are finite; a program needn't handle non-finite values.
Results may differ from a plain program's by a relative error of at most 0.0041.
Values may be sent and summed in bfloat16 or wider, within the bound.
No kernel may reach another device: no remote copies, remote signals or barrier semaphores. Data moves between devices by JAX's collectives and lax.ppermute only.
A program may use at most 64 MiB of HBM per device.

v0:
```python
import jax
import jax.numpy as jnp
from jax import lax
from jax.sharding import PartitionSpec as P

beta_one = 0.95
beta_two = 0.95
bias_one = 1.0 - 0.95**10
bias_two = 1.0 - 0.95**10
epsilon = 1e-08


def on_device(grad, right_basis, left_basis, first_moment, second_moment):
    shard_rows, shard_cols = grad.shape
    column_blocks = right_basis.shape[0]
    row_blocks = left_basis.shape[0]
    block_size = right_basis.shape[2]
    owner_rows, owner_cols = first_moment.shape
    grad_blocks = grad.reshape(shard_rows, column_blocks, block_size)
    right_whole = lax.all_gather(right_basis, "dp", axis=1, tiled=True)
    left_whole = lax.all_gather(left_basis, "dp", axis=1, tiled=True)
    turned = jnp.einsum(
        "rki,kio->rko", grad_blocks, right_whole, preferred_element_type=jnp.float32
    )
    rotated_cols = turned.reshape(shard_rows, shard_cols).astype(jnp.bfloat16)
    by_owners = lax.all_to_all(
        lax.all_to_all(rotated_cols, "dp", split_axis=1, concat_axis=0, tiled=True),
        "mp",
        split_axis=0,
        concat_axis=1,
        tiled=True,
    )
    owned = by_owners.reshape(row_blocks, block_size, owner_cols)
    rotated = jnp.einsum("bio,bic->boc", left_whole, owned, preferred_element_type=jnp.float32)
    eigen_grad = rotated.reshape(owner_rows, owner_cols)
    first_new = beta_one * first_moment + (1.0 - beta_one) * eigen_grad
    second_new = beta_two * second_moment + (1.0 - beta_two) * eigen_grad * eigen_grad
    direction = (first_new / bias_one / (jnp.sqrt(second_new / bias_two) + epsilon)).astype(
        jnp.bfloat16
    )
    direction_blocks = direction.reshape(row_blocks, block_size, owner_cols)
    back_rows = jnp.einsum(
        "bio,boc->bic", left_whole, direction_blocks, preferred_element_type=jnp.float32
    ).astype(jnp.bfloat16)
    back_owned = back_rows.reshape(owner_rows, owner_cols)
    by_rows = lax.all_to_all(
        lax.all_to_all(back_owned, "mp", split_axis=1, concat_axis=0, tiled=True),
        "dp",
        split_axis=0,
        concat_axis=1,
        tiled=True,
    )
    back_blocks = by_rows.reshape(shard_rows, column_blocks, block_size)
    update = jnp.einsum(
        "rko,kio->rki", back_blocks, right_whole, preferred_element_type=jnp.float32
    )
    return (update.reshape(shard_rows, shard_cols), first_new, second_new)


def solution(mesh):
    in_specs = (
        P("dp", "mp"),
        P("mp", "dp", None),
        P("mp", "dp", None),
        P("mp", "dp"),
        P("mp", "dp"),
    )
    out_specs = (P("dp", "mp"), P("mp", "dp"), P("mp", "dp"))
    return jax.shard_map(
        on_device, mesh=mesh, in_specs=in_specs, out_specs=out_specs, check_vma=False
    )
```

profile of v0, /device:TPU:1, one launch (start us, length us, event | category | flops | bytes accessed | tf_op | source)
XLA Modules:
  0.0 862.6 jit_solution(7654961164519464609)
XLA Ops:
  7.2 0.0 all-gather.3.cloned.1.call-start
  7.2 0.7 all-gather.3.cloned.1.call-update
  7.9 0.0 all-gather.5.cloned.1.call-start
  7.9 0.7 all-gather.5.cloned.1.call-update
  8.6 322.9 %all-gather.3.cloned.1.call-done = bf16[2,1024,1024]{2,1,0:T(8,128)(2,1)} async-done(((bf16[2,16,1024]{2,1,0:T(8,128)(2,1)}), bf16[2,1024,1024]{2,1,0:T(8,128)(2,1)}) %all-gather.3.cloned.1.call-update) | async-done | bytes 4194320 | tf_op jit(solution)/shard_map/all_gather | solution.py:20
  331.6 4.2 convolution_convert_fusion
  335.8 27.8 %all_to_all.61 = bf16[256,64,32]{0,2,1:T(8,128)(2,1)S(1)} all-to-all(bf16[256,64,32]{0,2,1:T(8,128)(2,1)S(1)} %bitcast.46), channel_id=1, replica_groups=mesh['dp'=64,'mp'=4] {'dp'}, dimensions={1} | all-to-all | bytes 2097152 | tf_op jit(solution)/shard_map/all_to_all | solution.py:27
  363.6 0.6 copy.23
  364.2 0.8 all_to_all.48
  365.0 0.6 copy.24
  365.6 98.5 %all_to_all.62 = bf16[4,4096,32]{1,2,0:T(8,128)(2,1)S(1)} all-to-all(bf16[4,4096,32]{1,2,0:T(8,128)(2,1)S(1)} %copy.24), channel_id=1, replica_groups=mesh['dp'=64,'mp'=4] {'mp'}, dimensions={0} | all-to-all | bytes 2097152 | tf_op jit(solution)/shard_map/all_to_all | solution.py:26
  464.1 0.8 reshape.46
  464.9 258.9 %all-gather.5.cloned.1.call-done = bf16[4,1024,1024]{2,1,0:T(8,128)(2,1)} async-done(((bf16[4,16,1024]{2,1,0:T(8,128)(2,1)}), bf16[4,1024,1024]{2,1,0:T(8,128)(2,1)}) %all-gather.5.cloned.1.call-update) | async-done | bytes 8388624 | tf_op jit(solution)/shard_map/all_gather | solution.py:21
  723.7 6.4 convolution_bitcast_fusion.1
  730.2 1.9 copy.26
  732.1 5.8 divide_convert_fusion
  737.9 6.3 fusion.1
  744.2 0.8 copy.28
  745.0 0.8 all_to_all.51
  745.8 68.2 %all_to_all.63 = bf16[4096,4,32]{0,2,1:T(8,128)(2,1)S(1)} all-to-all(bf16[4096,4,32]{0,2,1:T(8,128)(2,1)S(1)} %all_to_all.51), channel_id=1, replica_groups=mesh['dp'=64,'mp'=4] {'mp'}, dimensions={1} | all-to-all | bytes 2097152 | tf_op jit(solution)/shard_map/all_to_all | solution.py:47
  814.0 0.8 copy.29
  814.9 0.8 all_to_all.54
  815.6 0.0 copy-start
  815.6 0.6 copy.30
  816.2 33.4 %all_to_all.64 = bf16[64,256,32]{1,2,0:T(8,128)(2,1)S(1)} all-to-all(bf16[64,256,32]{1,2,0:T(8,128)(2,1)S(1)} %copy.30), channel_id=1, replica_groups=mesh['dp'=64,'mp'=4] {'dp'}, dimensions={0} | all-to-all | bytes 2097152 | tf_op jit(solution)/shard_map/all_to_all | solution.py:46
  849.6 0.0 copy-done
  849.6 1.4 convolution_bitcast_fusion
  851.0 1.9 copy.32
  852.9 2.9 copy.33
Async XLA Ops:
  7.2 324.4 %all-gather.3.cloned.1.call-start = ((), (), s32[]{:S(2)}) async-start(), calls=%async_computation.4 | async-start | bytes 4259840 | tf_op jit(solution)/shard_map/all_gather | solution.py:20
  7.9 715.9 %all-gather.5.cloned.1.call-start = ((), (), s32[]{:S(2)}) async-start(), calls=%async_computation.5 | async-start | bytes 8519680 | tf_op jit(solution)/shard_map/all_gather | solution.py:21
  815.6 34.0 %copy-start = (bf16[2,1024,1024]{2,1,0:T(8,128)(2,1)S(1)}, bf16[2,1024,1024]{2,1,0:T(8,128)(2,1)}, u32[]{:S(2)}) copy-start(bf16[2,1024,1024]{2,1,0:T(8,128)(2,1)} %all-gather.3.cloned.1.call-done) | copy-start | bytes 12582916
Sparse Core Ops, SparseCore 0:
  9.8 321.7 all-gather.2
  333.3 390.3 all-gather.4
where the time goes:
time: 863 us
  waiting for transfers between devices  583 us (68%)
  blocking collectives  228 us (26%)
  matrix products  18.3 us (2%)
  between operations  14.1 us (2%)
  local copies, waits for them, and re-layouts  13.2 us (2%)
    all_gather x1, waiting for transfers between devices, on_device(): right_whole = lax.all_gather(right_basis, 'dp', axis=1, tiled=True)  323 us
    all_gather x1, waiting for transfers between devices, on_device(): left_whole = lax.all_gather(left_basis, 'dp', axis=1, tiled=True)  259 us
    all_to_all x1, blocking collectives, on_device(): lax.all_to_all(lax.all_to_all(rotated_cols, 'dp', split_axis=1, concat_ax...  98.5 us
    all_to_all x1, blocking collectives, on_device(): lax.all_to_all(back_owned, 'mp', split_axis=1, concat_axis=0, tiled=True)  68.2 us
    all_to_all x1, blocking collectives, on_device(): lax.all_to_all(lax.all_to_all(back_owned, 'mp', split_axis=1, concat_axis...  33.4 us
    all_to_all x1, blocking collectives, on_device(): lax.all_to_all(rotated_cols, 'dp', split_axis=1, concat_axis=0, tiled=True)  27.8 us
  transfers between devices with their start and end apart: 2, of which 2 were waited for; matrix products, arithmetic and copies ran while one was open for 1% of the time, Pallas kernels for 0%

commit v1 on v0

v1 whole, which is shorter than its diff:
```python
import jax
import jax.numpy as jnp
from jax import lax
from jax.sharding import Mesh, PartitionSpec as P

beta_one = 0.95
beta_two = 0.95
bias_one = 1.0 - 0.95**10
bias_two = 1.0 - 0.95**10
epsilon = 1e-08

XY = ("x", "y")
ZC = ("zl", "zh", "core")


def gather_basis(shard):
    blocks, rows, width = shard.shape
    line = lax.all_gather(shard.reshape(blocks * rows, width), "zl", axis=0, tiled=True)
    whole = lax.all_gather(line, XY, axis=0, tiled=True)
    whole = whole.reshape(64, blocks, rows, width).transpose(1, 0, 2, 3)
    return whole.reshape(blocks, 64 * rows, width)


def on_device(grad, right_basis, left_basis, first_moment, second_moment):
    right_whole = gather_basis(right_basis)
    left_whole = gather_basis(left_basis)
    turned = jnp.einsum(
        "rki,kio->kor",
        grad.reshape(256, 2, 1024),
        right_whole,
        preferred_element_type=jnp.float32,
    ).astype(jnp.bfloat16)
    sent = turned.reshape(16, 128, 256)
    crossed = lax.all_to_all(sent, XY, split_axis=0, concat_axis=0, tiled=True)
    pieces = crossed.reshape(4, 4, 4, 32, 256).transpose(2, 0, 1, 3, 4).reshape(16, 128, 256)
    owned = lax.all_to_all(pieces, ZC, split_axis=0, concat_axis=0, tiled=True)
    owned = owned.reshape(4, 4, 4, 32, 256).transpose(2, 1, 3, 0, 4).reshape(4, 128, 1024)
    eigen_grad = jnp.einsum(
        "bio,bci->boc", left_whole, owned, preferred_element_type=jnp.float32
    ).reshape(4096, 128)
    first_new = beta_one * first_moment + (1.0 - beta_one) * eigen_grad
    second_new = beta_two * second_moment + (1.0 - beta_two) * eigen_grad * eigen_grad
    direction = (first_new / bias_one / (jnp.sqrt(second_new / bias_two) + epsilon)).astype(
        jnp.bfloat16
    )
    back = jnp.einsum(
        "bio,boc->bci",
        left_whole,
        direction.reshape(4, 1024, 128),
        preferred_element_type=jnp.float32,
    ).astype(jnp.bfloat16)
    back = back.reshape(4, 4, 32, 4, 256).transpose(3, 1, 0, 2, 4).reshape(16, 128, 256)
    back = lax.all_to_all(back, ZC, split_axis=0, concat_axis=0, tiled=True)
    back = back.reshape(4, 4, 4, 32, 256).transpose(1, 2, 0, 3, 4).reshape(16, 128, 256)
    back = lax.all_to_all(back, XY, split_axis=0, concat_axis=0, tiled=True)
    update = jnp.einsum(
        "kor,kio->rki",
        back.reshape(2, 1024, 256),
        right_whole,
        preferred_element_type=jnp.float32,
    )
    return update.reshape(256, 2048), first_new, second_new


def solution(mesh):
    fine = Mesh(mesh.devices.reshape(4, 4, 4, 2, 2), ("x", "y", "zl", "zh", "core"))
    dp, mp = ("x", "y", "zl"), ("zh", "core")
    in_specs = (P(dp, mp), P(mp, dp, None), P(mp, dp, None), P(mp, dp), P(mp, dp))
    out_specs = (P(dp, mp), P(mp, dp), P(mp, dp))
    return jax.shard_map(
        on_device, mesh=fine, in_specs=in_specs, out_specs=out_specs, check_vma=False
    )
```

time: 863 us -> 265 us (0.31)
  waiting for transfers between devices: 583 us -> 60 us
  blocking collectives: 228 us -> 148 us
    all_gather x2, waiting for transfers between devices: 582 us -> 60 us  [gather_basis(): whole = lax.all_gather(line, XY, axis=0, tiled=True)]
    all_to_all x4, blocking collectives: 228 us -> 119 us  [the longest x1 40 us: on_device(): owned = lax.all_to_all(pieces, ZC, split_axis=0, concat_axis=0, tiled=True)]
    all_gather x0 -> x2, blocking collectives: none -> 28.7 us  [gather_basis(): lax.all_gather(shard.reshape(blocks * rows, width), 'zl', axis=0, tiled=T...]
    transpose x1 -> x5, local copies, waits for them, and re-layouts: 1.88 us -> 14.1 us  [the longest x2 11.2 us: gather_basis(): whole = whole.reshape(64, blocks, rows, width).transpose(1, 0, 2, 3)]
  transfers between devices with their start and end apart: 2 -> 2, of which waited for: 2 -> 2; matrix products, arithmetic and copies ran while one was open for 1% -> 2% of each run, Pallas kernels for 0% -> 0%
where the time goes in v1:
time: 265 us; the launch traced here: 264 us
  blocking collectives  148 us (56%)
  waiting for transfers between devices  60 us (23%)
  local copies, waits for them, and re-layouts  20.8 us (8%)
  matrix products  15.5 us (6%)
  between operations  14.1 us (5%)
  other arithmetic  5.78 us (2%)
    all_gather x2, waiting for transfers between devices, gather_basis(): whole = lax.all_gather(line, XY, axis=0, tiled=True)  60 us
    all_to_all x1, blocking collectives, on_device(): owned = lax.all_to_all(pieces, ZC, split_axis=0, concat_axis=0, tiled=True)  40 us
    all_to_all x1, blocking collectives, on_device(): back = lax.all_to_all(back, ZC, split_axis=0, concat_axis=0, tiled=True)  35.7 us
    all_gather x2, blocking collectives, gather_basis(): lax.all_gather(shard.reshape(blocks * rows, width), 'zl', axis=0, tiled=T...  28.7 us
    all_to_all x1, blocking collectives, on_device(): crossed = lax.all_to_all(sent, XY, split_axis=0, concat_axis=0, tiled=True)  22.5 us
    all_to_all x1, blocking collectives, on_device(): back = lax.all_to_all(back, XY, split_axis=0, concat_axis=0, tiled=True)  20.9 us
    transpose x2, local copies, waits for them, and re-layouts, gather_basis(): whole = whole.reshape(64, blocks, rows, width).transpose(1, 0, 2, 3)  11.2 us
    dot_general x1, matrix products, on_device(): jnp.einsum('bio,boc->bci', left_whole, direction.reshape(4, 1024, 128), p...  6.29 us
  transfers between devices with their start and end apart: 2, of which 2 were waited for; matrix products, arithmetic and copies ran while one was open for 2% of the time, Pallas kernels for 0%

profile of v1, /device:TPU:1, one launch (start us, length us, event | category | flops | bytes accessed | tf_op | source)
XLA Modules:
  0.0 264.2 jit_solution(8581805373526741902)
XLA Ops:
  7.2 0.0 all-gather.3.cloned.1.call-start
  7.2 15.5 %all_gather.12 = bf16[128,1024]{1,0:T(8,128)(2,1)} all-gather(bf16[32,1024]{1,0:T(8,128)(2,1)} %bitcast.65), channel_id=1, replica_groups=mesh['x'=4,'y'=4,'zl'=4,'zh'=2,'core'=2] {'zl'}, dimensions={0}, use_global_device_ids=true | all-gather | bytes 327680 | tf_op jit(solution)/shard_map/all_gather | solution.py:18
  22.7 0.0 all-gather.3.cloned.1.call-update
  22.7 0.0 all-gather.5.cloned.1.call-start
  22.8 13.2 %all_gather.14 = bf16[256,1024]{1,0:T(8,128)(2,1)} all-gather(bf16[64,1024]{1,0:T(8,128)(2,1)} %bitcast.64), channel_id=1, replica_groups=mesh['x'=4,'y'=4,'zl'=4,'zh'=2,'core'=2] {'zl'}, dimensions={0}, use_global_device_ids=true | all-gather | bytes 655360 | tf_op jit(solution)/shard_map/all_gather | solution.py:18
  36.0 0.0 all-gather.5.cloned.1.call-update
  36.0 46.5 %all-gather.3.cloned.1.call-done = bf16[2048,1024]{1,0:T(8,128)(2,1)} async-done(((bf16[128,1024]{1,0:T(8,128)(2,1)}), bf16[2048,1024]{1,0:T(8,128)(2,1)}) %all-gather.3.cloned.1.call-update) | async-done | bytes 4194320 | tf_op jit(solution)/shard_map/all_gather | solution.py:19
  82.6 2.7 %copy.23 = bf16[2,64,16,1024]{3,2,1,0:T(8,128)(2,1)S(1)} copy(bf16[2,64,16,1024]{3,2,0,1:T(8,128)(2,1)} %bitcast.55) | data formatting | bytes 8388608 | tf_op jit(solution)/shard_map/transpose | solution.py:20
  85.3 0.0 copy-start
  85.3 0.0 copy-done.2
  85.3 1.8 convolution_convert_fusion
  87.1 0.1 copy-done
  87.2 22.5 %all_to_all.20 = bf16[16,128,256]{2,1,0:T(8,128)(2,1)S(1)} all-to-all(bf16[16,128,256]{2,1,0:T(8,128)(2,1)S(1)} %bitcast.63), channel_id=1, replica_groups=mesh['x'=4,'y'=4,'zl'=4,'zh'=2,'core'=2] {'x','y'}, dimensions={0} | all-to-all | bytes 2097152 | tf_op jit(solution)/shard_map/all_to_all | solution.py:34
  109.7 0.1 copy.26
  109.8 40.0 %all_to_all.21 = bf16[16,128,256]{2,1,0:T(8,128)(2,1)S(1)} all-to-all(bf16[16,128,256]{2,1,0:T(8,128)(2,1)S(1)} %bitcast.57), channel_id=1, replica_groups=mesh['x'=4,'y'=4,'zl'=4,'zh'=2,'core'=2] {'zl','zh','core'}, dimensions={0} | all-to-all | bytes 2097152 | tf_op jit(solution)/shard_map/all_to_all | solution.py:36
  149.9 0.9 copy.27
  150.8 0.8 reshape.74
  151.5 13.5 %all-gather.5.cloned.1.call-done = bf16[4096,1024]{1,0:T(8,128)(2,1)} async-done(((bf16[256,1024]{1,0:T(8,128)(2,1)}), bf16[4096,1024]{1,0:T(8,128)(2,1)}) %all-gather.5.cloned.1.call-update) | async-done | bytes 8388624 | tf_op jit(solution)/shard_map/all_gather | solution.py:19
  165.0 8.5 %copy.28 = bf16[4,64,16,1024]{3,2,1,0:T(8,128)(2,1)} copy(bf16[4,64,16,1024]{3,2,0,1:T(8,128)(2,1)} %bitcast.52) | data formatting | bytes 16777216 | tf_op jit(solution)/shard_map/transpose | solution.py:20
  173.6 6.0 %convolution_bitcast_fusion.1 = f32[4,1024,128]{1,2,0:T(8,128)} fusion(bf16[4,128,1024]{2,1,0:T(8,128)(2,1)S(1)} %reshape.74, bf16[4,1024,1024]{2,1,0:T(8,128)(2,1)} %bitcast.48), kind=kOutput, calls=%fused_computation.5 | convolution fusion | flops 1073741824 | bytes 11534336 | tf_op jit(solution)/shard_map/bio,bci->boc/dot_general | solution.py:38
  179.5 1.9 copy.29
  181.4 5.8 %divide_convert_fusion = (bf16[4096,128]{1,0:T(8,128)(2,1)S(1)}, f32[4096,128]{1,0:T(8,128)}, f32[4096,128]{1,0:T(8,128)}) fusion(f32[4,1024,128]{2,1,0:T(8,128)S(1)} %copy.29, f32[4096,128]{1,0:T(8,128)} %param.8, f32[4096,128]{1,0:T(8,128)} %param.9), kind=kLoop, calls=%fused_computation.3 | loop fusion | flops 5767168 | bytes 11534336 | tf_op jit(solution)/shard_map/convert_element_type | solution.py:43
  187.2 6.3 %convolution_convert_fusion.1 = bf16[4,128,1024]{2,1,0:T(8,128)(2,1)S(1)} fusion(bf16[4,1024,128]{2,1,0:T(8,128)(2,1)S(1)} %bitcast.62, bf16[4,1024,1024]{2,1,0:T(8,128)(2,1)} %bitcast.49), kind=kOutput, calls=%fused_computation.7 | convolution fusion | flops 1074266112 | bytes 10485760 | tf_op jit(solution)/shard_map/bio,boc->bci/dot_general | solution.py:46
  193.5 0.8 reshape.80
  194.3 0.2 copy.31
  194.5 35.7 %all_to_all.22 = bf16[16,128,256]{2,1,0:T(8,128)(2,1)S(1)} all-to-all(bf16[16,128,256]{2,1,0:T(8,128)(2,1)S(1)} %bitcast.59), channel_id=1, replica_groups=mesh['x'=4,'y'=4,'zl'=4,'zh'=2,'core'=2] {'zl','zh','core'}, dimensions={0} | all-to-all | bytes 2097152 | tf_op jit(solution)/shard_map/all_to_all | solution.py:53
  230.2 0.1 copy.32
  230.3 20.9 %all_to_all.23 = bf16[16,128,256]{2,1,0:T(8,128)(2,1)S(1)} all-to-all(bf16[16,128,256]{2,1,0:T(8,128)(2,1)S(1)} %bitcast.61), channel_id=1, replica_groups=mesh['x'=4,'y'=4,'zl'=4,'zh'=2,'core'=2] {'x','y'}, dimensions={0} | all-to-all | bytes 2097152 | tf_op jit(solution)/shard_map/all_to_all | solution.py:55
  251.2 0.0 copy-done.1
  251.2 1.4 convolution_bitcast_fusion
  252.6 1.9 copy.34
  254.5 2.9 %copy.35 = f32[256,2048]{1,0:T(8,128)} copy(f32[256,2048]{0,1:T(8,128)} %bitcast.53) | data formatting | bytes 4194304
  (2 shorter events, 0.0 us)
Async XLA Ops:
  7.2 75.4 %all-gather.3.cloned.1.call-start = ((), (), s32[]{:S(2)}) async-start(), calls=%async_computation.4 | async-start | bytes 4456448 | tf_op jit(solution)/shard_map/all_gather | solution.py:19
  22.7 142.3 %all-gather.5.cloned.1.call-start = ((), (), s32[]{:S(2)}) async-start(), calls=%async_computation.5 | async-start | bytes 8912896 | tf_op jit(solution)/shard_map/all_gather | solution.py:19
  82.6 2.7 %copy-start.2 = (bf16[256,2048]{1,0:T(8,128)(2,1)S(1)}, bf16[256,2048]{1,0:T(8,128)(2,1)}, u32[]{:S(2)}) copy-start(bf16[256,2048]{1,0:T(8,128)(2,1)} %param.5) | copy-start | bytes 3145732
  85.3 1.9 copy-start
  230.2 21.0 %copy-start.1 = (bf16[2,64,16,1024]{3,2,1,0:T(8,128)(2,1)S(1)}, bf16[2,64,16,1024]{3,2,1,0:T(8,128)(2,1)}, u32[]{:S(2)}) copy-start(bf16[2,64,16,1024]{3,2,1,0:T(8,128)(2,1)} %copy-done) | copy-start | bytes 12582916
Sparse Core Ops, SparseCore 0:
  22.8 59.6 all-gather.2
  85.0 79.9 all-gather.4

commit v2 on v1

v2 whole, which is shorter than its diff:
```python
import jax
import jax.numpy as jnp
from jax import lax
from jax.experimental import pallas as pl
from jax.experimental.pallas import tpu as pltpu
from jax.sharding import Mesh, PartitionSpec as P

beta_one = 0.95
beta_two = 0.95
bias_one = 1.0 - 0.95**10
bias_two = 1.0 - 0.95**10
epsilon = 1e-08

XY = ("x", "y")
ZC = ("zl", "zh", "core")
NEAR = (0, -1, 1, 2)
BLOCK = 1024
ROWS = 256
VMEM_LIMIT = 32 * 1024 * 1024


def shift(value, axis, by):
    return lax.ppermute(value, axis, [(i, (i + by) % 4) for i in range(4)])


def line_gather(shard, zl):
    held = [shard] + [shift(shard, "zl", t) for t in (1, 2, 3)]
    ordered = []
    for at in range(4):
        back = (zl - at) & 3
        ordered.append(
            jnp.where(
                back < 2,
                jnp.where(back == 0, held[0], held[1]),
                jnp.where(back == 2, held[2], held[3]),
            )
        )
    return jnp.stack(ordered, axis=-3).reshape(*shard.shape[:-2], 64, BLOCK)


def rings(first, second, first_axis, second_axis):
    pairs = [(first, second)]
    for by in (1, -1, 2):
        pairs.append((shift(first, first_axis, by), shift(second, second_axis, by)))
    return [pair[0] for pair in pairs], [pair[1] for pair in pairs]


def chip_row(place, half, outer, inner):
    to_x, to_y = (inner, outer) if half == 0 else (outer, inner)
    chip = ((place[0] + to_x + 4) & 3) * 4 + ((place[1] + to_y + 4) & 3)
    return pl.multiple_of(chip * 64, 64)


def first_kernel(place, grad, *refs):
    pieces, (sent, right_whole) = refs[:8], refs[8:]

    for k in range(2):

        @pl.when(pl.program_id(0) == k)
        def _():
            for piece in range(4):
                for at in range(4):
                    row = chip_row(place, k, NEAR[piece], NEAR[at])
                    right_whole[0, pl.ds(row, 64), :] = pieces[4 * k + piece][at]

    turned = jnp.dot(grad[...], right_whole[0], preferred_element_type=jnp.float32)
    sent[...] = turned.astype(jnp.bfloat16).T.reshape(8, 128, ROWS)


def first_stage(place, grad, pieces):
    return pl.pallas_call(
        first_kernel,
        out_shape=(
            jax.ShapeDtypeStruct((16, 128, ROWS), jnp.bfloat16),
            jax.ShapeDtypeStruct((2, BLOCK, BLOCK), jnp.bfloat16),
        ),
        grid_spec=pltpu.PrefetchScalarGridSpec(
            num_scalar_prefetch=1,
            grid=(2,),
            in_specs=[pl.BlockSpec((ROWS, BLOCK), lambda k, place: (0, k))]
            + [pl.BlockSpec((4, 64, BLOCK), lambda k, place: (0, 0, 0))] * len(pieces),
            out_specs=(
                pl.BlockSpec((8, 128, ROWS), lambda k, place: (k, 0, 0)),
                pl.BlockSpec((1, BLOCK, BLOCK), lambda k, place: (k, 0, 0)),
            ),
        ),
        compiler_params=pltpu.CompilerParams(vmem_limit_bytes=VMEM_LIMIT),
        cost_estimate=pl.CostEstimate(
            flops=2 * ROWS * 2 * BLOCK * BLOCK, bytes_accessed=10 * 2**20, transcendentals=0
        ),
        name="rotate_columns",
    )(place, grad, *pieces)


def middle_kernel(owned, left_block, first, second, back, first_out, second_out):
    left = left_block[:, 0].reshape(BLOCK, BLOCK)
    columns = jnp.concatenate(
        [owned[4 * z : 4 * z + 4, 0].reshape(128, ROWS) for z in range(4)], axis=1
    )
    eigen_grad = jnp.dot(columns, left, preferred_element_type=jnp.float32).T
    first_new = beta_one * first[...] + (1.0 - beta_one) * eigen_grad
    second_new = beta_two * second[...] + (1.0 - beta_two) * eigen_grad * eigen_grad
    first_out[...] = first_new
    second_out[...] = second_new
    direction = first_new / bias_one / (jnp.sqrt(second_new / bias_two) + epsilon)
    turned = lax.dot_general(
        direction.astype(jnp.bfloat16).T,
        left,
        (((1,), (1,)), ((), ())),
        preferred_element_type=jnp.float32,
    ).astype(jnp.bfloat16)
    for z in range(4):
        back[4 * z : 4 * z + 4, 0] = turned[:, z * ROWS : (z + 1) * ROWS].reshape(4, 32, ROWS)


def middle_stage(owned, left_whole, first_moment, second_moment):
    pieces = pl.BlockSpec((16, 1, 32, ROWS), lambda b: (0, b, 0, 0))
    moments = pl.BlockSpec((BLOCK, 128), lambda b: (b, 0))
    return pl.pallas_call(
        middle_kernel,
        out_shape=(
            jax.ShapeDtypeStruct((16, 4, 32, ROWS), jnp.bfloat16),
            jax.ShapeDtypeStruct((4 * BLOCK, 128), jnp.float32),
            jax.ShapeDtypeStruct((4 * BLOCK, 128), jnp.float32),
        ),
        grid=(4,),
        in_specs=[
            pieces,
            pl.BlockSpec((16, 1, 64, BLOCK), lambda b: (0, b, 0, 0)),
            moments,
            moments,
        ],
        out_specs=(pieces, moments, moments),
        compiler_params=pltpu.CompilerParams(vmem_limit_bytes=VMEM_LIMIT),
        cost_estimate=pl.CostEstimate(
            flops=4 * 4 * BLOCK * BLOCK * 128,
            bytes_accessed=18 * 2**20,
            transcendentals=4 * BLOCK * 128,
        ),
        name="moments_and_direction",
    )(owned, left_whole, first_moment, second_moment)


def last_kernel(back, right_whole, update):
    update[...] = lax.dot_general(
        back[...].reshape(BLOCK, ROWS).T,
        right_whole[0],
        (((1,), (1,)), ((), ())),
        preferred_element_type=jnp.float32,
    )


def last_stage(back, right_whole):
    return pl.pallas_call(
        last_kernel,
        out_shape=jax.ShapeDtypeStruct((ROWS, 2 * BLOCK), jnp.float32),
        grid=(2, 2),
        in_specs=[
            pl.BlockSpec((8, 128, ROWS), lambda k, i: (k, 0, 0)),
            pl.BlockSpec((1, BLOCK // 2, BLOCK), lambda k, i: (k, i, 0)),
        ],
        out_specs=pl.BlockSpec((ROWS, BLOCK // 2), lambda k, i: (0, 2 * k + i)),
        compiler_params=pltpu.CompilerParams(vmem_limit_bytes=VMEM_LIMIT),
        cost_estimate=pl.CostEstimate(
            flops=2 * ROWS * 2 * BLOCK * BLOCK, bytes_accessed=7 * 2**20, transcendentals=0
        ),
        name="rotate_back_columns",
    )(back, right_whole)


def on_device(grad, right_basis, left_basis, first_moment, second_moment):
    place = jnp.stack([lax.axis_index(axis) for axis in ("x", "y", "zl")]).astype(jnp.int32)
    zl = place[2]
    line = line_gather(jnp.concatenate([right_basis, left_basis]), zl)
    left_whole = lax.all_gather(line[2:].reshape(256, BLOCK), XY, axis=0, tiled=True)
    left_whole = left_whole.reshape(16, 4, 64, BLOCK)
    right_x, right_y = rings(line[0], line[1], "x", "y")
    right_x, right_y = lax.optimization_barrier((jnp.stack(right_x), jnp.stack(right_y)))
    right_x, right_y = rings(right_x, right_y, "y", "x")
    sent, right_whole = first_stage(place, grad, right_x + right_y)
    crossed = lax.all_to_all(sent, XY, split_axis=0, concat_axis=0, tiled=True)
    crossed = crossed.reshape(4, 4, 4, 32, ROWS).transpose(2, 0, 1, 3, 4).reshape(16, 128, ROWS)
    owned = lax.all_to_all(crossed, ZC, split_axis=0, concat_axis=0, tiled=True)
    left_whole, first_moment, second_moment = (
        pltpu.with_memory_space_constraint(value, pltpu.HBM)
        for value in (left_whole, first_moment, second_moment)
    )
    back, first_new, second_new = middle_stage(
        owned.reshape(16, 4, 32, ROWS), left_whole, first_moment, second_moment
    )
    back = lax.all_to_all(
        back.reshape(16, 128, ROWS), ZC, split_axis=0, concat_axis=0, tiled=True
    )
    back = back.reshape(4, 4, 4, 32, ROWS).transpose(1, 2, 0, 3, 4).reshape(16, 128, ROWS)
    back = lax.all_to_all(back, XY, split_axis=0, concat_axis=0, tiled=True)
    return last_stage(back, right_whole), first_new, second_new


def solution(mesh):
    fine = Mesh(mesh.devices.reshape(4, 4, 4, 2, 2), ("x", "y", "zl", "zh", "core"))
    dp, mp = ("x", "y", "zl"), ("zh", "core")
    in_specs = (P(dp, mp), P(mp, dp, None), P(mp, dp, None), P(mp, dp), P(mp, dp))
    out_specs = (P(dp, mp), P(mp, dp), P(mp, dp))
    return jax.shard_map(
        on_device, mesh=fine, in_specs=in_specs, out_specs=out_specs, check_vma=False
    )
```

time: 265 us -> 226 us (0.85)
  blocking collectives: 148 us -> 121 us
  starting transfers between devices: 0.08 us -> 19.3 us
  local copies, waits for them, and re-layouts: 20.8 us -> 1.94 us
  Pallas kernels: 0 us -> 17.2 us
  matrix products: 15.5 us -> 0 us
  waiting for transfers between devices: 60 us -> 50.4 us
  other arithmetic: 5.78 us -> 1.2 us
    all_gather x2 -> x1, waiting for transfers between devices: 60 us -> 0.01 us  [on_device(): lax.all_gather(line[2:].reshape(256, BLOCK), XY, axis=0, tiled=True)]
    ppermute x0 -> x15, waiting for transfers between devices: none -> 50.4 us  [shift(): return lax.ppermute(value, axis, [(i, (i + by) % 4) for i in range(4)])]
    all_gather x2 -> x0, blocking collectives: 28.7 us -> none  [gather_basis(): lax.all_gather(shard.reshape(blocks * rows, width), 'zl', axis=0, tiled=T...]
    ppermute x0 -> x15, starting transfers between devices: none -> 19.3 us  [shift(): return lax.ppermute(value, axis, [(i, (i + by) % 4) for i in range(4)])]
    pallas_call x0 -> x3, Pallas kernels: none -> 17.2 us  [the longest x1 10.1 us: middle_stage(): pl.pallas_call(middle_kernel, out_shape=(jax.ShapeDtypeStruct((16, 4, 32,...]
    dot_general x4 -> x0, matrix products: 15.5 us -> none  [the longest x1 6.29 us: on_device(): jnp.einsum('bio,boc->bci', left_whole, direction.reshape(4, 1024, 128), p...]
    transpose x5 -> x2, local copies, waits for them, and re-layouts: 14.1 us -> 0.17 us  [the longest x1 0.09 us: on_device(): back.reshape(4, 4, 4, 32, ROWS).transpose(1, 2, 0, 3, 4)]
    all_to_all x1, blocking collectives: 22.5 us -> 30.2 us  [on_device(): crossed = lax.all_to_all(sent, XY, split_axis=0, concat_axis=0, tiled=True)]
  transfers between devices with their start and end apart: 2 -> 16, of which waited for: 2 -> 9; matrix products, arithmetic and copies ran while one was open for 2% -> 0% of each run, Pallas kernels for 0% -> 2%
where the time goes in v2:
time: 226 us
  blocking collectives  121 us (54%)
  waiting for transfers between devices  50.4 us (22%)
  starting transfers between devices  19.3 us (9%)
  Pallas kernels  17.2 us (8%)
  between operations  14.1 us (6%)
    ppermute x15, waiting for transfers between devices, shift(): return lax.ppermute(value, axis, [(i, (i + by) % 4) for i in range(4)])  50.4 us
    all_to_all x1, blocking collectives, on_device(): owned = lax.all_to_all(crossed, ZC, split_axis=0, concat_axis=0, tiled=True)  38.8 us
    all_to_all x1, blocking collectives, on_device(): lax.all_to_all(back.reshape(16, 128, ROWS), ZC, split_axis=0, concat_axis...  31.2 us
    all_to_all x1, blocking collectives, on_device(): crossed = lax.all_to_all(sent, XY, split_axis=0, concat_axis=0, tiled=True)  30.2 us
    all_to_all x1, blocking collectives, on_device(): back = lax.all_to_all(back, XY, split_axis=0, concat_axis=0, tiled=True)  21.2 us
    ppermute x15, starting transfers between devices, shift(): return lax.ppermute(value, axis, [(i, (i + by) % 4) for i in range(4)])  19.3 us
    pallas_call x1, Pallas kernels, middle_stage(): pl.pallas_call(middle_kernel, out_shape=(jax.ShapeDtypeStruct((16, 4, 32,...  10.1 us
  transfers between devices with their start and end apart: 16, of which 9 were waited for; matrix products, arithmetic and copies ran while one was open for 0% of the time, Pallas kernels for 2%

profile of v2, /device:TPU:1, one launch (start us, length us, event | category | flops | bytes accessed | tf_op | source)
XLA Modules:
  0.0 225.6 jit_solution(6860375419795322511)
XLA Ops:
  7.2 0.8 constant_dynamic-update-slice_fusion.1
  8.1 0.9 constant_dynamic-update-slice_fusion
  9.0 5.3 %collective-permute-start.2 = (bf16[6,16,1024]{2,1,0:T(8,128)(2,1)S(1)}, bf16[6,16,1024]{2,1,0:T(8,128)(2,1)S(1)}, u32[]{:S(2)}, u32[]{:S(2)}) collective-permute-start(bf16[6,16,1024]{2,1,0:T(8,128)(2,1)S(1)} %constant_dynamic-update-slice_fusion), channel_id=1, source_target_pairs={{0,12},{4,0},{8,4},{12,8},{1,13},{5,1},{9,5},{13,9},{2,14},{6,2},{... | collective-permute-start | bytes 589832 | tf_op jit(solution)/shard_map/ppermute | solution.py:23
  14.2 0.4 collective-permute-start
  14.6 3.3 %collective-permute-done.2 = bf16[6,16,1024]{2,1,0:T(8,128)(2,1)S(1)} collective-permute-done((bf16[6,16,1024]{2,1,0:T(8,128)(2,1)S(1)}, bf16[6,16,1024]{2,1,0:T(8,128)(2,1)S(1)}, u32[]{:S(2)}, u32[]{:S(2)}) %collective-permute-start.2) | collective-permute-done | bytes 196640 | tf_op jit(solution)/shard_map/ppermute | solution.py:23
  17.9 12.3 %collective-permute-done.1 = bf16[6,16,1024]{2,1,0:T(8,128)(2,1)S(1)} collective-permute-done((bf16[6,16,1024]{2,1,0:T(8,128)(2,1)S(1)}, bf16[6,16,1024]{2,1,0:T(8,128)(2,1)S(1)}, u32[]{:S(2)}, u32[]{:S(2)}) %collective-permute-start.1) | collective-permute-done | bytes 196640 | tf_op jit(solution)/shard_map/ppermute | solution.py:23
  30.4 0.9 pad_maximum_fusion
  31.3 2.8 %collective-permute-start.5 = (bf16[64,1024]{1,0:T(8,128)(2,1)S(1)}, bf16[64,1024]{1,0:T(8,128)(2,1)S(1)}, u32[]{:S(2)}, u32[]{:S(2)}) collective-permute-start(bf16[64,1024]{1,0:T(8,128)(2,1)S(1)} %bitcast.51), channel_id=1, source_target_pairs={{0,128},{64,192},{128,0},{192,64},{1,129},{65,193},{129,1},{193,65... | collective-permute-start | bytes 393224 | tf_op jit(solution)/shard_map/ppermute | solution.py:23
  34.1 0.9 collective-permute-start.4
  35.0 0.6 collective-permute-start.3
  35.6 2.9 %collective-permute-start.8 = (bf16[64,1024]{1,0:T(8,128)(2,1)S(1)}, bf16[64,1024]{1,0:T(8,128)(2,1)S(1)}, u32[]{:S(2)}, u32[]{:S(2)}) collective-permute-start(bf16[64,1024]{1,0:T(8,128)(2,1)S(1)} %bitcast.47), channel_id=1, source_target_pairs={{0,32},{16,48},{32,0},{48,16},{1,33},{17,49},{33,1},{49,17},{2,34}... | collective-permute-start | bytes 393224 | tf_op jit(solution)/shard_map/ppermute | solution.py:23
  38.5 0.8 collective-permute-start.7
  39.3 0.7 collective-permute-start.6
  40.0 0.4 collective-permute-done.3
  40.5 0.4 collective-permute-done.8
  40.9 2.4 %collective-permute-done.7 = bf16[64,1024]{1,0:T(8,128)(2,1)S(1)} collective-permute-done((bf16[64,1024]{1,0:T(8,128)(2,1)S(1)}, bf16[64,1024]{1,0:T(8,128)(2,1)S(1)}, u32[]{:S(2)}, u32[]{:S(2)}) %collective-permute-start.7) | collective-permute-done | bytes 131104 | tf_op jit(solution)/shard_map/ppermute | solution.py:23
  43.3 1.9 collective-permute-done.6
  45.3 0.8 collective-permute-start.11
  46.1 1.0 collective-permute-start.10
  47.1 0.4 collective-permute-start.9
  47.6 2.0 collective-permute-start.14
  49.6 0.7 collective-permute-start.13
  50.3 13.5 %collective-permute-done.11.refs_3_ = bf16[4,64,1024]{2,1,0:T(8,128)(2,1)S(1)} collective-permute-done((bf16[4,64,1024]{2,1,0:T(8,128)(2,1)S(1)}, bf16[4,64,1024]{2,1,0:T(8,128)(2,1)S(1)}, u32[]{:S(2)}, u32[]{:S(2)}) %collective-permute-start.11) | collective-permute-done | bytes 524320 | tf_op jit(solution)/shard_map/ppermute | solution.py:23
  63.9 13.2 %collective-permute-done.10.refs_2_ = bf16[4,64,1024]{2,1,0:T(8,128)(2,1)S(1)} collective-permute-done((bf16[4,64,1024]{2,1,0:T(8,128)(2,1)S(1)}, bf16[4,64,1024]{2,1,0:T(8,128)(2,1)S(1)}, u32[]{:S(2)}, u32[]{:S(2)}) %collective-permute-start.10) | collective-permute-done | bytes 524320 | tf_op jit(solution)/shard_map/ppermute | solution.py:23
  77.1 2.8 %collective-permute-done.9.refs_1_ = bf16[4,64,1024]{2,1,0:T(8,128)(2,1)} collective-permute-done((bf16[4,64,1024]{2,1,0:T(8,128)(2,1)S(1)}, bf16[4,64,1024]{2,1,0:T(8,128)(2,1)}, u32[]{:S(2)}, u32[]{:S(2)}) %collective-permute-start.9) | collective-permute-done | bytes 524320 | tf_op jit(solution)/shard_map/ppermute | solution.py:23
  79.9 4.1 %rotate_columns.1 = (bf16[16,128,256]{2,1,0:T(8,128)(2,1)S(1)}, bf16[2,1024,1024]{2,1,0:T(8,128)(2,1)S(1)}) custom-call(s32[3]{0:T(128)S(1)} %pad_add_fusion.place, bf16[256,2048]{1,0:T(8,128)(2,1)S(1)} %copy-done.2, bf16[4,64,1024]{2,1,0:T(8,128)(2,1)S(1)} %pad_maximum_fusion.3.refs_0_, bf16[4,64,1024]{2,1,0:T(8,128)(2,1)} %collective-permute-done.9.refs_1_, ...), custom_call_target="tpu_custom_call" | custom-call | flops 1073741824 | bytes 10485760 | tf_op jit(solution)/shard_map/rotate_columns/pallas_call | solution.py:71
  84.0 30.2 %all_to_all.20 = bf16[16,128,256]{2,1,0:T(8,128)(2,1)S(1)} all-to-all(bf16[16,128,256]{2,1,0:T(8,128)(2,1)S(1)} %get-tuple-element.12), channel_id=1, replica_groups=mesh['x'=4,'y'=4,'zl'=4,'zh'=2,'core'=2] {'x','y'}, dimensions={0} | all-to-all | bytes 2097152 | tf_op jit(solution)/shard_map/all_to_all | solution.py:181
  114.3 38.8 %all_to_all.21 = bf16[16,128,256]{2,1,0:T(8,128)(2,1)S(1)} all-to-all(bf16[16,128,256]{2,1,0:T(8,128)(2,1)S(1)} %bitcast.43), channel_id=1, replica_groups=mesh['x'=4,'y'=4,'zl'=4,'zh'=2,'core'=2] {'zl','zh','core'}, dimensions={0} | all-to-all | bytes 2097152 | tf_op jit(solution)/shard_map/all_to_all | solution.py:183
  153.1 10.1 %moments_and_direction.1 = (bf16[16,4,32,256]{3,2,1,0:T(8,128)(2,1)S(1)}, f32[4096,128]{1,0:T(8,128)}, f32[4096,128]{1,0:T(8,128)}) custom-call(bf16[16,4,32,256]{3,2,1,0:T(8,128)(2,1)S(1)} %bitcast.39, bf16[16,4,64,1024]{3,2,1,0:T(8,128)(2,1)} %bitcast.41, f32[4096,128]{1,0:T(8,128)} %first.1, f32[4096,128]{1,0:T(8,128)} %second.1), custom_call_target="tpu_custom_call" | custom-call | flops 2147483648 | bytes 18874368 | tf_op jit(solution)/shard_map/moments_and_direction/pallas_call | solution.py:119
  163.2 31.2 %all_to_all.22 = bf16[16,128,256]{2,1,0:T(8,128)(2,1)S(1)} all-to-all(bf16[16,128,256]{2,1,0:T(8,128)(2,1)S(1)} %bitcast.40), channel_id=1, replica_groups=mesh['x'=4,'y'=4,'zl'=4,'zh'=2,'core'=2] {'zl','zh','core'}, dimensions={0} | all-to-all | bytes 2097152 | tf_op jit(solution)/shard_map/all_to_all | solution.py:191
  194.5 21.2 %all_to_all.23.back = bf16[16,128,256]{2,1,0:T(8,128)(2,1)S(1)} all-to-all(bf16[16,128,256]{2,1,0:T(8,128)(2,1)S(1)} %bitcast.45), channel_id=1, replica_groups=mesh['x'=4,'y'=4,'zl'=4,'zh'=2,'core'=2] {'x','y'}, dimensions={0} | all-to-all | bytes 2097152 | tf_op jit(solution)/shard_map/all_to_all | solution.py:195
  215.7 3.0 %rotate_back_columns.1 = f32[256,2048]{1,0:T(8,128)} custom-call(bf16[16,128,256]{2,1,0:T(8,128)(2,1)S(1)} %all_to_all.23.back, bf16[2,1024,1024]{2,1,0:T(8,128)(2,1)S(1)} %copy-done.1), custom_call_target="tpu_custom_call" | custom-call | flops 1073741824 | bytes 7340032 | tf_op jit(solution)/shard_map/rotate_back_columns/pallas_call | solution.py:154
  (24 shorter events, 0.6 us)
Async XLA Ops:
  7.2 145.9 %all-gather.2.cloned.1.call-start = ((), (), s32[]{:S(2)}) async-start(), calls=%async_computation.4 | async-start | bytes 8912896 | tf_op jit(solution)/shard_map/all_gather | solution.py:175
  9.0 9.0 %collective-permute-start.2 = (bf16[6,16,1024]{2,1,0:T(8,128)(2,1)S(1)}, bf16[6,16,1024]{2,1,0:T(8,128)(2,1)S(1)}, u32[]{:S(2)}, u32[]{:S(2)}) collective-permute-start(bf16[6,16,1024]{2,1,0:T(8,128)(2,1)S(1)} %constant_dynamic-update-slice_fusion), channel_id=1, source_target_pairs={{0,12},{4,0},{8,4},{12,8},{1,13},{5,1},{9,5},{13,9},{2,14},{6,2},{... | collective-permute-start | bytes 589832 | tf_op jit(solution)/shard_map/ppermute | solution.py:23
  14.2 16.0 %collective-permute-start.1 = (bf16[6,16,1024]{2,1,0:T(8,128)(2,1)S(1)}, bf16[6,16,1024]{2,1,0:T(8,128)(2,1)S(1)}, u32[]{:S(2)}, u32[]{:S(2)}) collective-permute-start(bf16[6,16,1024]{2,1,0:T(8,128)(2,1)S(1)} %constant_dynamic-update-slice_fusion), channel_id=1, source_target_pairs={{0,8},{4,12},{8,0},{12,4},{1,9},{5,13},{9,1},{13,5},{2,10},{6,14},... | collective-permute-start | bytes 589832 | tf_op jit(solution)/shard_map/ppermute | solution.py:23
  14.2 16.0 %collective-permute-start = (bf16[6,16,1024]{2,1,0:T(8,128)(2,1)S(1)}, bf16[6,16,1024]{2,1,0:T(8,128)(2,1)S(1)}, u32[]{:S(2)}, u32[]{:S(2)}) collective-permute-start(bf16[6,16,1024]{2,1,0:T(8,128)(2,1)S(1)} %constant_dynamic-update-slice_fusion), channel_id=1, source_target_pairs={{0,4},{4,8},{8,12},{12,0},{1,5},{5,9},{9,13},{13,1},{2,6},{6,10},{... | collective-permute-start | bytes 589832 | tf_op jit(solution)/shard_map/ppermute | solution.py:23
  31.2 48.7 %copy-start.2 = (bf16[256,2048]{1,0:T(8,128)(2,1)S(1)}, bf16[256,2048]{1,0:T(8,128)(2,1)}, u32[]{:S(2)}) copy-start(bf16[256,2048]{1,0:T(8,128)(2,1)} %grad.1) | copy-start | bytes 3145732
  31.3 8.0 %collective-permute-start.5 = (bf16[64,1024]{1,0:T(8,128)(2,1)S(1)}, bf16[64,1024]{1,0:T(8,128)(2,1)S(1)}, u32[]{:S(2)}, u32[]{:S(2)}) collective-permute-start(bf16[64,1024]{1,0:T(8,128)(2,1)S(1)} %bitcast.51), channel_id=1, source_target_pairs={{0,128},{64,192},{128,0},{192,64},{1,129},{65,193},{129,1},{193,65... | collective-permute-start | bytes 393224 | tf_op jit(solution)/shard_map/ppermute | solution.py:23
  34.1 5.9 %collective-permute-start.4 = (bf16[64,1024]{1,0:T(8,128)(2,1)S(1)}, bf16[64,1024]{1,0:T(8,128)(2,1)S(1)}, u32[]{:S(2)}, u32[]{:S(2)}) collective-permute-start(bf16[64,1024]{1,0:T(8,128)(2,1)S(1)} %bitcast.52), channel_id=1, source_target_pairs={{0,192},{64,0},{128,64},{192,128},{1,193},{65,1},{129,65},{193,129... | collective-permute-start | bytes 393224 | tf_op jit(solution)/shard_map/ppermute | solution.py:23
  35.0 5.4 %collective-permute-start.3 = (bf16[64,1024]{1,0:T(8,128)(2,1)S(1)}, bf16[64,1024]{1,0:T(8,128)(2,1)S(1)}, u32[]{:S(2)}, u32[]{:S(2)}) collective-permute-start(bf16[64,1024]{1,0:T(8,128)(2,1)S(1)} %bitcast.53), channel_id=1, source_target_pairs={{0,64},{64,128},{128,192},{192,0},{1,65},{65,129},{129,193},{193,1... | collective-permute-start | bytes 393224 | tf_op jit(solution)/shard_map/ppermute | solution.py:23
  35.6 5.3 %collective-permute-start.8 = (bf16[64,1024]{1,0:T(8,128)(2,1)S(1)}, bf16[64,1024]{1,0:T(8,128)(2,1)S(1)}, u32[]{:S(2)}, u32[]{:S(2)}) collective-permute-start(bf16[64,1024]{1,0:T(8,128)(2,1)S(1)} %bitcast.47), channel_id=1, source_target_pairs={{0,32},{16,48},{32,0},{48,16},{1,33},{17,49},{33,1},{49,17},{2,34}... | collective-permute-start | bytes 393224 | tf_op jit(solution)/shard_map/ppermute | solution.py:23
  38.5 4.8 %collective-permute-start.7 = (bf16[64,1024]{1,0:T(8,128)(2,1)S(1)}, bf16[64,1024]{1,0:T(8,128)(2,1)S(1)}, u32[]{:S(2)}, u32[]{:S(2)}) collective-permute-start(bf16[64,1024]{1,0:T(8,128)(2,1)S(1)} %bitcast.48), channel_id=1, source_target_pairs={{0,48},{16,0},{32,16},{48,32},{1,49},{17,1},{33,17},{49,33},{2,50}... | collective-permute-start | bytes 393224 | tf_op jit(solution)/shard_map/ppermute | solution.py:23
  39.3 5.9 %collective-permute-start.6 = (bf16[64,1024]{1,0:T(8,128)(2,1)S(1)}, bf16[64,1024]{1,0:T(8,128)(2,1)S(1)}, u32[]{:S(2)}, u32[]{:S(2)}) collective-permute-start(bf16[64,1024]{1,0:T(8,128)(2,1)S(1)} %bitcast.49), channel_id=1, source_target_pairs={{0,16},{16,32},{32,48},{48,0},{1,17},{17,33},{33,49},{49,1},{2,18}... | collective-permute-start | bytes 393224 | tf_op jit(solution)/shard_map/ppermute | solution.py:23
  45.3 18.5 %collective-permute-start.11 = (bf16[4,64,1024]{2,1,0:T(8,128)(2,1)S(1)}, bf16[4,64,1024]{2,1,0:T(8,128)(2,1)S(1)}, u32[]{:S(2)}, u32[]{:S(2)}) collective-permute-start(bf16[4,64,1024]{2,1,0:T(8,128)(2,1)S(1)} %pad_maximum_fusion.3.refs_0_), channel_id=1, source_target_pairs={{0,32},{16,48},{32,0},{48,16},{1,33},{17,49},{33,1},{49,17},{2,34}... | collective-permute-start | bytes 1572872 | tf_op jit(solution)/shard_map/ppermute | solution.py:23
  46.1 31.0 %collective-permute-start.10 = (bf16[4,64,1024]{2,1,0:T(8,128)(2,1)S(1)}, bf16[4,64,1024]{2,1,0:T(8,128)(2,1)S(1)}, u32[]{:S(2)}, u32[]{:S(2)}) collective-permute-start(bf16[4,64,1024]{2,1,0:T(8,128)(2,1)S(1)} %pad_maximum_fusion.3.refs_0_), channel_id=1, source_target_pairs={{0,48},{16,0},{32,16},{48,32},{1,49},{17,1},{33,17},{49,33},{2,50}... | collective-permute-start | bytes 1572872 | tf_op jit(solution)/shard_map/ppermute | solution.py:23
  47.1 32.8 %collective-permute-start.9 = (bf16[4,64,1024]{2,1,0:T(8,128)(2,1)S(1)}, bf16[4,64,1024]{2,1,0:T(8,128)(2,1)}, u32[]{:S(2)}, u32[]{:S(2)}) collective-permute-start(bf16[4,64,1024]{2,1,0:T(8,128)(2,1)S(1)} %pad_maximum_fusion.3.refs_0_), channel_id=1, source_target_pairs={{0,16},{16,32},{32,48},{48,0},{1,17},{17,33},{33,49},{49,1},{2,18}... | collective-permute-start | bytes 1572872 | tf_op jit(solution)/shard_map/ppermute | solution.py:23
  47.6 32.3 %collective-permute-start.14 = (bf16[4,64,1024]{2,1,0:T(8,128)(2,1)S(1)}, bf16[4,64,1024]{2,1,0:T(8,128)(2,1)}, u32[]{:S(2)}, u32[]{:S(2)}) collective-permute-start(bf16[4,64,1024]{2,1,0:T(8,128)(2,1)S(1)} %pad_maximum_fusion.4.refs_4_), channel_id=1, source_target_pairs={{0,128},{64,192},{128,0},{192,64},{1,129},{65,193},{129,1},{193,65... | collective-permute-start | bytes 1572872 | tf_op jit(solution)/shard_map/ppermute | solution.py:23
  49.6 30.3 %collective-permute-start.13 = (bf16[4,64,1024]{2,1,0:T(8,128)(2,1)S(1)}, bf16[4,64,1024]{2,1,0:T(8,128)(2,1)}, u32[]{:S(2)}, u32[]{:S(2)}) collective-permute-start(bf16[4,64,1024]{2,1,0:T(8,128)(2,1)S(1)} %pad_maximum_fusion.4.refs_4_), channel_id=1, source_target_pairs={{0,192},{64,0},{128,64},{192,128},{1,193},{65,1},{129,65},{193,129... | collective-permute-start | bytes 1572872 | tf_op jit(solution)/shard_map/ppermute | solution.py:23
  63.8 16.1 %collective-permute-start.12 = (bf16[4,64,1024]{2,1,0:T(8,128)(2,1)S(1)}, bf16[4,64,1024]{2,1,0:T(8,128)(2,1)}, u32[]{:S(2)}, u32[]{:S(2)}) collective-permute-start(bf16[4,64,1024]{2,1,0:T(8,128)(2,1)S(1)} %pad_maximum_fusion.4.refs_4_), channel_id=1, source_target_pairs={{0,64},{64,128},{128,192},{192,0},{1,65},{65,129},{129,193},{193,1... | collective-permute-start | bytes 1572872 | tf_op jit(solution)/shard_map/ppermute | solution.py:23
  84.0 30.3 %copy-start = (bf16[2,1024,1024]{2,1,0:T(8,128)(2,1)}, bf16[2,1024,1024]{2,1,0:T(8,128)(2,1)S(1)}, u32[]{:S(2)}) copy-start(bf16[2,1024,1024]{2,1,0:T(8,128)(2,1)S(1)} %get-tuple-element.14.right_whole) | copy-start | bytes 12582916
  194.4 21.3 %copy-start.1 = (bf16[2,1024,1024]{2,1,0:T(8,128)(2,1)S(1)}, bf16[2,1024,1024]{2,1,0:T(8,128)(2,1)}, u32[]{:S(2)}) copy-start(bf16[2,1024,1024]{2,1,0:T(8,128)(2,1)} %copy-done) | copy-start | bytes 12582916
Sparse Core Ops, SparseCore 0:
  31.4 104.1 all-gather.1

commit v3 on v2

v3 whole, which is shorter than its diff:
```python
import jax
import jax.numpy as jnp
from jax import lax
from jax.experimental import pallas as pl
from jax.experimental.pallas import tpu as pltpu
from jax.sharding import Mesh, PartitionSpec as P

beta_one = 0.95
beta_two = 0.95
bias_one = 1.0 - 0.95**10
bias_two = 1.0 - 0.95**10
epsilon = 1e-08

XY = ("x", "y")
ZC = ("zl", "zh", "core")
NEAR = (0, -1, 1, 2)
BLOCK = 1024
ROWS = 256
VMEM_LIMIT = 32 * 1024 * 1024


def shift(value, axis, by):
    return lax.ppermute(value, axis, [(i, (i + by) % 4) for i in range(4)])


def line_gather(shard, zl):
    held = [shard] + [shift(shard, "zl", t) for t in (1, 2, 3)]
    ordered = []
    for at in range(4):
        back = (zl - at) & 3
        ordered.append(
            jnp.where(
                back < 2,
                jnp.where(back == 0, held[0], held[1]),
                jnp.where(back == 2, held[2], held[3]),
            )
        )
    return jnp.stack(ordered, axis=-3).reshape(*shard.shape[:-2], 64, BLOCK)


def ring(axis, shard_for):
    return [shard_for(0)] + [shift(shard_for(by), axis, by) for by in (1, -1, 2)]


def first_kernel(place, kept, given, *refs):
    pieces, (sent, whole) = refs[:8], refs[8:]
    x, y, core = place[0], place[1], place[3]
    step = pl.program_id(0)

    @pl.when(step == 0)
    def _():
        for half in range(2):
            for outer in range(4):
                for inner in range(4):
                    to_x, to_y = (inner, outer) if half == 0 else (outer, inner)
                    chip = ((x + NEAR[to_x] + 4) & 3) * 4 + ((y + NEAR[to_y] + 4) & 3)
                    row = pl.multiple_of(chip * 64 + half * 32, 32)
                    whole[pl.ds(row, 32), :] = pieces[4 * half + outer][inner]

    rows = jnp.where(step == 0, kept[...], given[...])
    turned = jnp.dot(rows, whole[...], preferred_element_type=jnp.float32)
    turned = turned.astype(jnp.bfloat16).T
    for low in range(2):
        sent[low ^ core, :, 0] = turned[512 * low : 512 * low + 512].reshape(16, 32, ROWS)


def first_stage(place, kept, given, pieces):
    return pl.pallas_call(
        first_kernel,
        out_shape=jax.ShapeDtypeStruct((2, 16, 2, 32, ROWS), jnp.bfloat16),
        grid_spec=pltpu.PrefetchScalarGridSpec(
            num_scalar_prefetch=1,
            grid=(2,),
            in_specs=[pl.BlockSpec((ROWS, BLOCK), lambda g, place: (0, 0))] * 2
            + [pl.BlockSpec((4, 32, BLOCK), lambda g, place: (0, 0, 0))] * len(pieces),
            out_specs=pl.BlockSpec(
                (2, 16, 1, 32, ROWS), lambda g, place: (0, 0, (place[0] >> 1) ^ g, 0, 0)
            ),
            scratch_shapes=[pltpu.VMEM((BLOCK, BLOCK), jnp.bfloat16)],
        ),
        compiler_params=pltpu.CompilerParams(vmem_limit_bytes=VMEM_LIMIT),
        cost_estimate=pl.CostEstimate(
            flops=2 * ROWS * 2 * BLOCK * BLOCK, bytes_accessed=4 * 2**20, transcendentals=0
        ),
        name="rotate_columns",
    )(place, kept, given, *pieces)


def middle_kernel(place, owned, left_block, first, second, back, first_out, second_out):
    left = left_block[:, 0].reshape(BLOCK, BLOCK)
    low = place[0] & 1
    columns = jnp.concatenate(
        [
            jnp.concatenate(
                [owned[0, 4 * z + (q & 2) + ((q & 1) ^ low)] for q in range(4)], axis=0
            )
            for z in range(4)
        ],
        axis=1,
    )
    eigen_grad = jnp.dot(columns, left, preferred_element_type=jnp.float32).T
    first_new = beta_one * first[...] + (1.0 - beta_one) * eigen_grad
    second_new = beta_two * second[...] + (1.0 - beta_two) * eigen_grad * eigen_grad
    first_out[...] = first_new
    second_out[...] = second_new
    direction = first_new / bias_one / (jnp.sqrt(second_new / bias_two) + epsilon)
    turned = lax.dot_general(
        direction.astype(jnp.bfloat16).T,
        left,
        (((1,), (1,)), ((), ())),
        preferred_element_type=jnp.float32,
    ).astype(jnp.bfloat16)
    for z in range(4):
        back[4 * z : 4 * z + 4, 0] = turned[:, z * ROWS : (z + 1) * ROWS].reshape(4, 32, ROWS)


def middle_stage(place, owned, left_whole, first_moment, second_moment):
    pieces = pl.BlockSpec((16, 1, 32, ROWS), lambda b, place: (0, b, 0, 0))
    moments = pl.BlockSpec((BLOCK, 128), lambda b, place: (b, 0))
    return pl.pallas_call(
        middle_kernel,
        out_shape=(
            jax.ShapeDtypeStruct((16, 4, 32, ROWS), jnp.bfloat16),
            jax.ShapeDtypeStruct((4 * BLOCK, 128), jnp.float32),
            jax.ShapeDtypeStruct((4 * BLOCK, 128), jnp.float32),
        ),
        grid_spec=pltpu.PrefetchScalarGridSpec(
            num_scalar_prefetch=1,
            grid=(4,),
            in_specs=[
                pl.BlockSpec((1, 16, 32, ROWS), lambda b, place: (b, 0, 0, 0)),
                pl.BlockSpec((16, 1, 64, BLOCK), lambda b, place: (0, b, 0, 0)),
                moments,
                moments,
            ],
            out_specs=(pieces, moments, moments),
        ),
        compiler_params=pltpu.CompilerParams(vmem_limit_bytes=VMEM_LIMIT),
        cost_estimate=pl.CostEstimate(
            flops=4 * 4 * BLOCK * BLOCK * 128,
            bytes_accessed=18 * 2**20,
            transcendentals=4 * BLOCK * 128,
        ),
        name="moments_and_direction",
    )(place, owned, left_whole, first_moment, second_moment)


def last_kernel(back, right_whole, update):
    update[...] = lax.dot_general(
        back[...].reshape(BLOCK, ROWS).T,
        right_whole[:, 0].reshape(BLOCK // 2, BLOCK),
        (((1,), (1,)), ((), ())),
        preferred_element_type=jnp.float32,
    )


def last_stage(back, right_whole):
    return pl.pallas_call(
        last_kernel,
        out_shape=jax.ShapeDtypeStruct((ROWS, 2 * BLOCK), jnp.float32),
        grid=(2, 2),
        in_specs=[
            pl.BlockSpec((8, 128, ROWS), lambda k, i: (k, 0, 0)),
            pl.BlockSpec((8, 1, 64, BLOCK), lambda k, i: (i, k, 0, 0)),
        ],
        out_specs=pl.BlockSpec((ROWS, BLOCK // 2), lambda k, i: (0, 2 * k + i)),
        compiler_params=pltpu.CompilerParams(vmem_limit_bytes=VMEM_LIMIT),
        cost_estimate=pl.CostEstimate(
            flops=2 * ROWS * 2 * BLOCK * BLOCK, bytes_accessed=7 * 2**20, transcendentals=0
        ),
        name="rotate_back_columns",
    )(back, right_whole)


def gather_whole(line):
    whole = lax.all_gather(line.reshape(-1, BLOCK), XY, axis=0, tiled=True)
    return whole.reshape(16, *line.shape)


def on_device(grad, right_basis, left_basis, first_moment, second_moment):
    x, y, zl, core = (
        lax.axis_index(axis).astype(jnp.int32) for axis in ("x", "y", "zl", "core")
    )
    place = jnp.stack([x, y, zl, core])
    tie = lax.optimization_barrier

    def for_x(by, blocks):
        return jnp.where(((x + by) & 3) < 2, blocks[0], blocks[1])

    halves = grad[:, :BLOCK], grad[:, BLOCK:]
    kept = for_x(0, halves)
    given = lax.ppermute(for_x(2, halves), "x", [(i, i ^ 2) for i in range(4)])

    line = line_gather(jnp.concatenate([right_basis, left_basis]), zl)
    given, line = tie((given, line))
    left_whole = gather_whole(line[2:])
    right = line[0], line[1]
    by_x = jnp.stack(ring("x", lambda by: for_x(by, [block[:32] for block in right])))
    both = jnp.stack([block[32:] for block in right])
    by_y = jnp.stack(ring("y", lambda by: both))
    by_x, by_y = tie((by_x, by_y))
    pieces = ring("y", lambda by: by_x) + ring("x", lambda by: for_x(by, (by_y[:, 0], by_y[:, 1])))
    sent = first_stage(place, kept, given, pieces)

    moved = []
    for t in range(2):
        pairs = [
            (4 * high + 2 * low + c, 4 * high + 2 * (c ^ t) + low)
            for high in range(2)
            for low in range(2)
            for c in range(2)
        ]
        moved.append(lax.ppermute(sent[t], ("x", "core"), pairs))
    moved = jnp.stack(moved, axis=2).reshape(32, 64, ROWS)
    owned = lax.all_to_all(moved, ("y", "zl", "zh"), split_axis=0, concat_axis=0, tiled=True)
    owned = owned.reshape(4, 16, 32, ROWS)
    owned, right_line = tie((owned, line[:2]))
    right_whole = gather_whole(right_line)
    left_whole, first_moment, second_moment = (
        pltpu.with_memory_space_constraint(value, pltpu.HBM)
        for value in (left_whole, first_moment, second_moment)
    )
    back, first_new, second_new = middle_stage(
        place, owned, left_whole, first_moment, second_moment
    )
    back = lax.all_to_all(
        back.reshape(16, 128, ROWS), ZC, split_axis=0, concat_axis=0, tiled=True
    )
    back = back.reshape(4, 4, 4, 32, ROWS).transpose(1, 2, 0, 3, 4).reshape(16, 128, ROWS)
    back = lax.all_to_all(back, XY, split_axis=0, concat_axis=0, tiled=True)
    return last_stage(back, right_whole), first_new, second_new


def solution(mesh):
    fine = Mesh(mesh.devices.reshape(4, 4, 4, 2, 2), ("x", "y", "zl", "zh", "core"))
    dp, mp = ("x", "y", "zl"), ("zh", "core")
    in_specs = (P(dp, mp), P(mp, dp, None), P(mp, dp, None), P(mp, dp), P(mp, dp))
    out_specs = (P(dp, mp), P(mp, dp), P(mp, dp))
    return jax.shard_map(
        on_device, mesh=fine, in_specs=in_specs, out_specs=out_specs, check_vma=False
    )
```

time: 226 us -> 214 us (0.947)
  blocking collectives: 121 us -> 33.2 us
  waiting for transfers between devices: 50.4 us -> 91.3 us
  starting transfers between devices: 19.3 us -> 45.8 us
  local copies, waits for them, and re-layouts: 1.94 us -> 8.84 us
    all_to_all x3 -> x0, blocking collectives: 90.2 us -> none  [the longest x1 38.8 us: on_device(): owned = lax.all_to_all(crossed, ZC, split_axis=0, concat_axis=0, tiled=True)]
    all_to_all x0 -> x2, waiting for transfers between devices: none -> 38.2 us  [the longest x1 26.4 us: on_device(): lax.all_to_all(moved, ('y', 'zl', 'zh'), split_axis=0, concat_axis=0, til...]
    ppermute x15, waiting for transfers between devices: 50.4 us -> 29.2 us  [shift(): return lax.ppermute(value, axis, [(i, (i + by) % 4) for i in range(4)])]
    ppermute x0 -> x3, waiting for transfers between devices: none -> 19.8 us  [the longest x2 19.8 us: on_device(): moved.append(lax.ppermute(sent[t], ('x', 'core'), pairs))]
    all_to_all x0 -> x2, starting transfers between devices: none -> 14.6 us  [the longest x1 10.5 us: on_device(): lax.all_to_all(moved, ('y', 'zl', 'zh'), split_axis=0, concat_axis=0, til...]
    ppermute x0 -> x3, starting transfers between devices: none -> 8.43 us  [the longest x2 5.6 us: on_device(): moved.append(lax.ppermute(sent[t], ('x', 'core'), pairs))]
    all_gather x1 -> x2, waiting for transfers between devices: 0.01 us -> 4.12 us  [gather_whole(): whole = lax.all_gather(line.reshape(-1, BLOCK), XY, axis=0, tiled=True)]
    ppermute x15, starting transfers between devices: 19.3 us -> 22.7 us  [shift(): return lax.ppermute(value, axis, [(i, (i + by) % 4) for i in range(4)])]
  transfers between devices with their start and end apart: 16 -> 22, of which waited for: 9 -> 11; matrix products, arithmetic and copies ran while one was open for 0% -> 3% of each run, Pallas kernels for 2% -> 6%
where the time goes in v3:
time: 214 us; the launch traced here: 212 us
  waiting for transfers between devices  91.3 us (43%)
  starting transfers between devices  45.8 us (21%)
  blocking collectives  33.2 us (16%)
  Pallas kernels  16.2 us (8%)
  between operations  14.2 us (7%)
  local copies, waits for them, and re-layouts  8.84 us (4%)
  other arithmetic  2.66 us (1%)
    all_to_all x1, blocking collectives, on_device(): lax.all_to_all(back.reshape(16, 128, ROWS), ZC, split_axis=0, concat_axis...  33.2 us
    ppermute x15, waiting for transfers between devices, shift(): return lax.ppermute(value, axis, [(i, (i + by) % 4) for i in range(4)])  29.2 us
    all_to_all x1, waiting for transfers between devices, on_device(): lax.all_to_all(moved, ('y', 'zl', 'zh'), split_axis=0, concat_axis=0, til...  26.4 us
    ppermute x15, starting transfers between devices, shift(): return lax.ppermute(value, axis, [(i, (i + by) % 4) for i in range(4)])  22.7 us
    ppermute x2, waiting for transfers between devices, on_device(): moved.append(lax.ppermute(sent[t], ('x', 'core'), pairs))  19.8 us
    all_to_all x1, waiting for transfers between devices, on_device(): back = lax.all_to_all(back, XY, split_axis=0, concat_axis=0, tiled=True)  11.8 us
    pallas_call x1, Pallas kernels, middle_stage(): pl.pallas_call(middle_kernel, out_shape=(jax.ShapeDtypeStruct((16, 4, 32,...  10.6 us
    all_to_all x1, starting transfers between devices, on_device(): lax.all_to_all(moved, ('y', 'zl', 'zh'), split_axis=0, concat_axis=0, til...  10.5 us
  transfers between devices with their start and end apart: 22, of which 11 were waited for; matrix products, arithmetic and copies ran while one was open for 3% of the time, Pallas kernels for 6%

profile of v3, /device:TPU:1, one launch (start us, length us, event | category | flops | bytes accessed | tf_op | source)
XLA Modules:
  0.0 212.3 jit_solution(11923114468824546848)
XLA Ops:
  9.0 5.3 %collective-permute-start.3 = (bf16[6,16,1024]{2,1,0:T(8,128)(2,1)S(1)}, bf16[6,16,1024]{2,1,0:T(8,128)(2,1)S(1)}, u32[]{:S(2)}, u32[]{:S(2)}) collective-permute-start(bf16[6,16,1024]{2,1,0:T(8,128)(2,1)S(1)} %constant_dynamic-update-slice_fusion), channel_id=1, source_target_pairs={{0,12},{4,0},{8,4},{12,8},{1,13},{5,1},{9,5},{13,9},{2,14},{6,2},{... | collective-permute-start | bytes 589832 | tf_op jit(solution)/shard_map/ppermute | solution.py:23
  14.6 1.3 broadcast_select_fusion
  15.9 2.8 %collective-permute-start = (bf16[256,1024]{1,0:T(8,128)(2,1)S(1)}, bf16[256,1024]{1,0:T(8,128)(2,1)S(1)}, u32[]{:S(2)}, u32[]{:S(2)}) collective-permute-start(bf16[256,1024]{1,0:T(8,128)(2,1)S(1)} %get-tuple-element.23), channel_id=1, source_target_pairs={{0,128},{64,192},{128,0},{192,64},{1,129},{65,193},{129,1},{193,65... | collective-permute-start | bytes 1572872 | tf_op jit(solution)/shard_map/ppermute | solution.py:192
  18.7 11.5 %collective-permute-done.2 = bf16[6,16,1024]{2,1,0:T(8,128)(2,1)S(1)} collective-permute-done((bf16[6,16,1024]{2,1,0:T(8,128)(2,1)S(1)}, bf16[6,16,1024]{2,1,0:T(8,128)(2,1)S(1)}, u32[]{:S(2)}, u32[]{:S(2)}) %collective-permute-start.2) | collective-permute-done | bytes 196640 | tf_op jit(solution)/shard_map/ppermute | solution.py:23
  31.6 2.6 %collective-permute-start.5 = (bf16[32,1024]{1,0:T(8,128)(2,1)S(1)}, bf16[32,1024]{1,0:T(8,128)(2,1)S(1)}, u32[]{:S(2)}, u32[]{:S(2)}) collective-permute-start(bf16[32,1024]{1,0:T(8,128)(2,1)S(1)} %get-tuple-element.28), channel_id=1, source_target_pairs={{0,192},{64,0},{128,64},{192,128},{1,193},{65,1},{129,65},{193,129... | collective-permute-start | bytes 196616 | tf_op jit(solution)/shard_map/ppermute | solution.py:23
  35.3 2.8 %collective-permute-start.8 = (bf16[2,32,1024]{2,1,0:T(8,128)(2,1)S(1)}, bf16[2,32,1024]{2,1,0:T(8,128)(2,1)S(1)}, u32[]{:S(2)}, u32[]{:S(2)}) collective-permute-start(bf16[2,32,1024]{2,1,0:T(8,128)(2,1)S(1)} %get-tuple-element.26), channel_id=1, source_target_pairs={{0,48},{16,0},{32,16},{48,32},{1,49},{17,1},{33,17},{49,33},{2,50}... | collective-permute-start | bytes 393224 | tf_op jit(solution)/shard_map/ppermute | solution.py:23
  38.1 1.6 collective-permute-start.9
  40.0 4.5 %collective-permute-done.7 = bf16[2,32,1024]{2,1,0:T(8,128)(2,1)S(1)} collective-permute-done((bf16[2,32,1024]{2,1,0:T(8,128)(2,1)S(1)}, bf16[2,32,1024]{2,1,0:T(8,128)(2,1)S(1)}, u32[]{:S(2)}, u32[]{:S(2)}) %collective-permute-start.7) | collective-permute-done | bytes 131104 | tf_op jit(solution)/shard_map/ppermute | solution.py:23
  44.6 1.2 collective-permute-start.12
  45.8 1.6 collective-permute-start.11
  48.2 2.1 %collective-permute-start.15 = (bf16[4,32,1024]{2,1,0:T(8,128)(2,1)}, bf16[4,32,1024]{2,1,0:T(8,128)(2,1)S(1)}, u32[]{:S(2)}, u32[]{:S(2)}) collective-permute-start(bf16[4,32,1024]{2,1,0:T(8,128)(2,1)} %get-tuple-element.35), channel_id=1, source_target_pairs={{0,128},{64,192},{128,0},{192,64},{1,129},{65,193},{129,1},{193,65... | collective-permute-start | bytes 786440 | tf_op jit(solution)/shard_map/ppermute | solution.py:23
  50.4 1.8 collective-permute-start.14
  52.2 2.3 %collective-permute-start.13 = (bf16[4,32,1024]{2,1,0:T(8,128)(2,1)S(1)}, bf16[4,32,1024]{2,1,0:T(8,128)(2,1)S(1)}, u32[]{:S(2)}, u32[]{:S(2)}) collective-permute-start(bf16[4,32,1024]{2,1,0:T(8,128)(2,1)S(1)} %get-tuple-element.38), channel_id=1, source_target_pairs={{0,64},{64,128},{128,192},{192,0},{1,65},{65,129},{129,193},{193,1... | collective-permute-start | bytes 786440 | tf_op jit(solution)/shard_map/ppermute | solution.py:23
  54.5 9.0 %collective-permute-done.11.refs_2_ = bf16[4,32,1024]{2,1,0:T(8,128)(2,1)S(1)} collective-permute-done((bf16[4,32,1024]{2,1,0:T(8,128)(2,1)S(1)}, bf16[4,32,1024]{2,1,0:T(8,128)(2,1)S(1)}, u32[]{:S(2)}, u32[]{:S(2)}) %collective-permute-start.11) | collective-permute-done | bytes 262176 | tf_op jit(solution)/shard_map/ppermute | solution.py:23
  63.6 1.5 collective-permute-done.10.refs_1_
  65.0 2.4 %collective-permute-done.14.refs_6_ = bf16[4,32,1024]{2,1,0:T(8,128)(2,1)S(1)} collective-permute-done((bf16[4,32,1024]{2,1,0:T(8,128)(2,1)}, bf16[4,32,1024]{2,1,0:T(8,128)(2,1)S(1)}, u32[]{:S(2)}, u32[]{:S(2)}) %collective-permute-start.14) | collective-permute-done | bytes 262176 | tf_op jit(solution)/shard_map/ppermute | solution.py:23
  67.4 2.4 %rotate_columns.1 = bf16[2,16,2,32,256]{4,3,2,1,0:T(8,128)(2,1)S(1)} custom-call(s32[4]{0:T(128)S(1)} %pad_add_fusion.place, bf16[256,1024]{1,0:T(8,128)(2,1)S(1)} %get-tuple-element.24.kept, bf16[256,1024]{1,0:T(8,128)(2,1)S(1)} %collective-permute-done.given, bf16[4,32,1024]{2,1,0:T(8,128)(2,1)S(1)} %pad_maximum_fusion.3.refs_0_, ...), custom_call_target="tpu_custom_call" | custom-call | flops 1073741824 | bytes 4194304 | tf_op jit(solution)/shard_map/rotate_columns/pallas_call | solution.py:68
  69.9 5.5 %collective-permute-start.16 = (bf16[16,2,32,256]{3,2,1,0:T(8,128)(2,1)S(1)}, bf16[16,2,32,256]{3,2,1,0:T(8,128)(2,1)S(1)}, u32[]{:S(2)}, u32[]{:S(2)}) collective-permute-start(bf16[16,2,32,256]{3,2,1,0:T(8,128)(2,1)S(1)} %get-tuple-element.21), channel_id=1, source_target_pairs={{0,0},{1,64},{64,1},{65,65},{128,128},{129,192},{192,129},{193,193... | collective-permute-start | bytes 1572872 | tf_op jit(solution)/shard_map/ppermute | solution.py:213
  75.6 17.0 %collective-permute-done.16 = bf16[16,2,32,256]{3,2,1,0:T(8,128)(2,1)S(1)} collective-permute-done((bf16[16,2,32,256]{3,2,1,0:T(8,128)(2,1)S(1)}, bf16[16,2,32,256]{3,2,1,0:T(8,128)(2,1)S(1)}, u32[]{:S(2)}, u32[]{:S(2)}) %collective-permute-start.16) | collective-permute-done | bytes 524320 | tf_op jit(solution)/shard_map/ppermute | solution.py:213
  92.5 2.8 %collective-permute-done.17 = bf16[16,2,32,256]{3,2,1,0:T(8,128)(2,1)S(1)} collective-permute-done((bf16[16,2,32,256]{3,2,1,0:T(8,128)(2,1)S(1)}, bf16[16,2,32,256]{3,2,1,0:T(8,128)(2,1)S(1)}, u32[]{:S(2)}, u32[]{:S(2)}) %collective-permute-start.17) | collective-permute-done | bytes 524320 | tf_op jit(solution)/shard_map/ppermute | solution.py:213
  95.4 1.1 copy.16
  96.5 10.5 %all-to-all-start = ((bf16[32,64,256]{2,1,0:T(8,128)(2,1)}), bf16[32,64,256]{2,1,0:T(8,128)(2,1)S(1)}, u32[]{:S(2)}, u32[]{:S(2)}) async-start(bf16[32,64,256]{2,1,0:T(8,128)(2,1)} %bitcast.30), calls=%async_computation | async-start | bytes 2097152 | tf_op jit(solution)/shard_map/all_to_all | solution.py:215
  107.1 1.7 slice.63
  108.8 26.4 %all-to-all-done = bf16[32,64,256]{2,1,0:T(8,128)(2,1)S(1)} async-done(((bf16[32,64,256]{2,1,0:T(8,128)(2,1)}), bf16[32,64,256]{2,1,0:T(8,128)(2,1)S(1)}, u32[]{:S(2)}, u32[]{:S(2)}) %all-to-all-start) | async-done | bytes 1048608 | tf_op jit(solution)/shard_map/all_to_all | solution.py:215
  135.2 10.6 %moments_and_direction.1 = (bf16[16,4,32,256]{3,2,1,0:T(8,128)(2,1)S(1)}, f32[4096,128]{1,0:T(8,128)}, f32[4096,128]{1,0:T(8,128)}) custom-call(s32[4]{0:T(128)S(1)} %pad_add_fusion.place, bf16[4,16,32,256]{3,2,1,0:T(8,128)(2,1)S(1)} %bitcast.59, bf16[16,4,64,1024]{3,2,1,0:T(8,128)(2,1)} %bitcast.61, f32[4096,128]{1,0:T(8,128)} %first.1, f32[4096,128]{1,0:T(8,128)} %second.1), custom_call_target="tpu_custom_call" | custom-call | flops 2147483648 | bytes 18874368 | tf_op jit(solution)/shard_map/moments_and_direction/pallas_call | solution.py:120
  145.8 33.2 %all_to_all.15 = bf16[16,128,256]{2,1,0:T(8,128)(2,1)S(1)} all-to-all(bf16[16,128,256]{2,1,0:T(8,128)(2,1)S(1)} %bitcast.60), channel_id=1, replica_groups=mesh['x'=4,'y'=4,'zl'=4,'zh'=2,'core'=2] {'zl','zh','core'}, dimensions={0} | all-to-all | bytes 2097152 | tf_op jit(solution)/shard_map/all_to_all | solution.py:226
  179.0 1.1 copy.17
  180.1 4.0 %all-to-all-start.2 = ((bf16[16,128,256]{2,1,0:T(8,128)(2,1)}), bf16[16,128,256]{2,1,0:T(8,128)(2,1)S(1)}, u32[]{:S(2)}, u32[]{:S(2)}) async-start(bf16[16,128,256]{2,1,0:T(8,128)(2,1)} %bitcast.37), calls=%async_computation.2 | async-start | bytes 2097152 | tf_op jit(solution)/shard_map/all_to_all | solution.py:230
  184.1 4.1 %all-gather.5.cloned.1.call-done = bf16[2048,1024]{1,0:T(8,128)(2,1)} async-done(((bf16[128,1024]{1,0:T(8,128)(2,1)}), bf16[2048,1024]{1,0:T(8,128)(2,1)}) %all-gather.5.cloned.1.call-update) | async-done | bytes 4194320 | tf_op jit(solution)/shard_map/all_gather | solution.py:176
  188.2 11.8 %all-to-all-done.2.back = bf16[16,128,256]{2,1,0:T(8,128)(2,1)S(1)} async-done(((bf16[16,128,256]{2,1,0:T(8,128)(2,1)}), bf16[16,128,256]{2,1,0:T(8,128)(2,1)S(1)}, u32[]{:S(2)}, u32[]{:S(2)}) %all-to-all-start.2) | async-done | bytes 1048608 | tf_op jit(solution)/shard_map/all_to_all | solution.py:230
  200.0 2.2 %copy-done = bf16[2048,1024]{1,0:T(8,128)(2,1)S(1)} copy-done((bf16[2048,1024]{1,0:T(8,128)(2,1)S(1)}, bf16[2048,1024]{1,0:T(8,128)(2,1)}, u32[]{:S(2)}) %copy-start) | copy-done | bytes 4194328
  202.2 3.3 %rotate_back_columns.1 = f32[256,2048]{1,0:T(8,128)} custom-call(bf16[16,128,256]{2,1,0:T(8,128)(2,1)S(1)} %all-to-all-done.2.back, bf16[16,2,64,1024]{3,2,1,0:T(8,128)(2,1)S(1)} %bitcast.58), custom_call_target="tpu_custom_call" | custom-call | flops 1073741824 | bytes 7340032 | tf_op jit(solution)/shard_map/rotate_back_columns/pallas_call | solution.py:158
  (40 shorter events, 6.2 us)
Async XLA Ops:
  7.2 128.1 %all-gather.3.cloned.1.call-start = ((), (), s32[]{:S(2)}) async-start(), calls=%async_computation.3 | async-start | bytes 8912896 | tf_op jit(solution)/shard_map/all_gather | solution.py:176
  9.0 9.7 %collective-permute-start.3 = (bf16[6,16,1024]{2,1,0:T(8,128)(2,1)S(1)}, bf16[6,16,1024]{2,1,0:T(8,128)(2,1)S(1)}, u32[]{:S(2)}, u32[]{:S(2)}) collective-permute-start(bf16[6,16,1024]{2,1,0:T(8,128)(2,1)S(1)} %constant_dynamic-update-slice_fusion), channel_id=1, source_target_pairs={{0,12},{4,0},{8,4},{12,8},{1,13},{5,1},{9,5},{13,9},{2,14},{6,2},{... | collective-permute-start | bytes 589832 | tf_op jit(solution)/shard_map/ppermute | solution.py:23
  14.2 16.0 %collective-permute-start.2 = (bf16[6,16,1024]{2,1,0:T(8,128)(2,1)S(1)}, bf16[6,16,1024]{2,1,0:T(8,128)(2,1)S(1)}, u32[]{:S(2)}, u32[]{:S(2)}) collective-permute-start(bf16[6,16,1024]{2,1,0:T(8,128)(2,1)S(1)} %constant_dynamic-update-slice_fusion), channel_id=1, source_target_pairs={{0,8},{4,12},{8,0},{12,4},{1,9},{5,13},{9,1},{13,5},{2,10},{6,14},... | collective-permute-start | bytes 589832 | tf_op jit(solution)/shard_map/ppermute | solution.py:23
  14.2 16.0 %collective-permute-start.1 = (bf16[6,16,1024]{2,1,0:T(8,128)(2,1)S(1)}, bf16[6,16,1024]{2,1,0:T(8,128)(2,1)S(1)}, u32[]{:S(2)}, u32[]{:S(2)}) collective-permute-start(bf16[6,16,1024]{2,1,0:T(8,128)(2,1)S(1)} %constant_dynamic-update-slice_fusion), channel_id=1, source_target_pairs={{0,4},{4,8},{8,12},{12,0},{1,5},{5,9},{9,13},{13,1},{2,6},{6,10},{... | collective-permute-start | bytes 589832 | tf_op jit(solution)/shard_map/ppermute | solution.py:23
  15.9 14.7 %collective-permute-start = (bf16[256,1024]{1,0:T(8,128)(2,1)S(1)}, bf16[256,1024]{1,0:T(8,128)(2,1)S(1)}, u32[]{:S(2)}, u32[]{:S(2)}) collective-permute-start(bf16[256,1024]{1,0:T(8,128)(2,1)S(1)} %get-tuple-element.23), channel_id=1, source_target_pairs={{0,128},{64,192},{128,0},{192,64},{1,129},{65,193},{129,1},{193,65... | collective-permute-start | bytes 1572872 | tf_op jit(solution)/shard_map/ppermute | solution.py:192
  30.5 14.0 %copy-start.1 = (bf16[6,4,16,1024]{3,2,1,0:T(8,128)(2,1)}, bf16[6,4,16,1024]{3,2,1,0:T(8,128)(2,1)S(1)}, u32[]{:S(2)}) copy-start(bf16[6,4,16,1024]{3,2,1,0:T(8,128)(2,1)S(1)} %copy.12) | copy-start | bytes 2359300
  31.6 6.5 %collective-permute-start.5 = (bf16[32,1024]{1,0:T(8,128)(2,1)S(1)}, bf16[32,1024]{1,0:T(8,128)(2,1)S(1)}, u32[]{:S(2)}, u32[]{:S(2)}) collective-permute-start(bf16[32,1024]{1,0:T(8,128)(2,1)S(1)} %get-tuple-element.28), channel_id=1, source_target_pairs={{0,192},{64,0},{128,64},{192,128},{1,193},{65,1},{129,65},{193,129... | collective-permute-start | bytes 196616 | tf_op jit(solution)/shard_map/ppermute | solution.py:23
  34.1 5.6 %collective-permute-start.6 = (bf16[32,1024]{1,0:T(8,128)(2,1)S(1)}, bf16[32,1024]{1,0:T(8,128)(2,1)S(1)}, u32[]{:S(2)}, u32[]{:S(2)}) collective-permute-start(bf16[32,1024]{1,0:T(8,128)(2,1)S(1)} %get-tuple-element.29), channel_id=1, source_target_pairs={{0,128},{64,192},{128,0},{192,64},{1,129},{65,193},{129,1},{193,65... | collective-permute-start | bytes 196616 | tf_op jit(solution)/shard_map/ppermute | solution.py:23
  34.6 5.1 %collective-permute-start.4 = (bf16[32,1024]{1,0:T(8,128)(2,1)S(1)}, bf16[32,1024]{1,0:T(8,128)(2,1)S(1)}, u32[]{:S(2)}, u32[]{:S(2)}) collective-permute-start(bf16[32,1024]{1,0:T(8,128)(2,1)S(1)} %get-tuple-element.30), channel_id=1, source_target_pairs={{0,64},{64,128},{128,192},{192,0},{1,65},{65,129},{129,193},{193,1... | collective-permute-start | bytes 196616 | tf_op jit(solution)/shard_map/ppermute | solution.py:23
  35.3 4.8 %collective-permute-start.8 = (bf16[2,32,1024]{2,1,0:T(8,128)(2,1)S(1)}, bf16[2,32,1024]{2,1,0:T(8,128)(2,1)S(1)}, u32[]{:S(2)}, u32[]{:S(2)}) collective-permute-start(bf16[2,32,1024]{2,1,0:T(8,128)(2,1)S(1)} %get-tuple-element.26), channel_id=1, source_target_pairs={{0,48},{16,0},{32,16},{48,32},{1,49},{17,1},{33,17},{49,33},{2,50}... | collective-permute-start | bytes 393224 | tf_op jit(solution)/shard_map/ppermute | solution.py:23
  38.1 6.4 %collective-permute-start.7 = (bf16[2,32,1024]{2,1,0:T(8,128)(2,1)S(1)}, bf16[2,32,1024]{2,1,0:T(8,128)(2,1)S(1)}, u32[]{:S(2)}, u32[]{:S(2)}) collective-permute-start(bf16[2,32,1024]{2,1,0:T(8,128)(2,1)S(1)} %get-tuple-element.26), channel_id=1, source_target_pairs={{0,16},{16,32},{32,48},{48,0},{1,17},{17,33},{33,49},{49,1},{2,18}... | collective-permute-start | bytes 393224 | tf_op jit(solution)/shard_map/ppermute | solution.py:23
  38.1 6.4 %collective-permute-start.9 = (bf16[2,32,1024]{2,1,0:T(8,128)(2,1)S(1)}, bf16[2,32,1024]{2,1,0:T(8,128)(2,1)S(1)}, u32[]{:S(2)}, u32[]{:S(2)}) collective-permute-start(bf16[2,32,1024]{2,1,0:T(8,128)(2,1)S(1)} %get-tuple-element.26), channel_id=1, source_target_pairs={{0,32},{16,48},{32,0},{48,16},{1,33},{17,49},{33,1},{49,17},{2,34}... | collective-permute-start | bytes 393224 | tf_op jit(solution)/shard_map/ppermute | solution.py:23
  44.6 7.6 %collective-permute-start.12 = (bf16[4,32,1024]{2,1,0:T(8,128)(2,1)S(1)}, bf16[4,32,1024]{2,1,0:T(8,128)(2,1)S(1)}, u32[]{:S(2)}, u32[]{:S(2)}) collective-permute-start(bf16[4,32,1024]{2,1,0:T(8,128)(2,1)S(1)} %pad_maximum_fusion.3.refs_0_), channel_id=1, source_target_pairs={{0,32},{16,48},{32,0},{48,16},{1,33},{17,49},{33,1},{49,17},{2,34}... | collective-permute-start | bytes 786440 | tf_op jit(solution)/shard_map/ppermute | solution.py:23
  45.8 17.8 %collective-permute-start.11 = (bf16[4,32,1024]{2,1,0:T(8,128)(2,1)S(1)}, bf16[4,32,1024]{2,1,0:T(8,128)(2,1)S(1)}, u32[]{:S(2)}, u32[]{:S(2)}) collective-permute-start(bf16[4,32,1024]{2,1,0:T(8,128)(2,1)S(1)} %pad_maximum_fusion.3.refs_0_), channel_id=1, source_target_pairs={{0,48},{16,0},{32,16},{48,32},{1,49},{17,1},{33,17},{49,33},{2,50}... | collective-permute-start | bytes 786440 | tf_op jit(solution)/shard_map/ppermute | solution.py:23
  47.4 17.7 %collective-permute-start.10 = (bf16[4,32,1024]{2,1,0:T(8,128)(2,1)S(1)}, bf16[4,32,1024]{2,1,0:T(8,128)(2,1)S(1)}, u32[]{:S(2)}, u32[]{:S(2)}) collective-permute-start(bf16[4,32,1024]{2,1,0:T(8,128)(2,1)S(1)} %pad_maximum_fusion.3.refs_0_), channel_id=1, source_target_pairs={{0,16},{16,32},{32,48},{48,0},{1,17},{17,33},{33,49},{49,1},{2,18}... | collective-permute-start | bytes 786440 | tf_op jit(solution)/shard_map/ppermute | solution.py:23
  48.2 16.8 %collective-permute-start.15 = (bf16[4,32,1024]{2,1,0:T(8,128)(2,1)}, bf16[4,32,1024]{2,1,0:T(8,128)(2,1)S(1)}, u32[]{:S(2)}, u32[]{:S(2)}) collective-permute-start(bf16[4,32,1024]{2,1,0:T(8,128)(2,1)} %get-tuple-element.35), channel_id=1, source_target_pairs={{0,128},{64,192},{128,0},{192,64},{1,129},{65,193},{129,1},{193,65... | collective-permute-start | bytes 786440 | tf_op jit(solution)/shard_map/ppermute | solution.py:23
  50.4 17.1 %collective-permute-start.14 = (bf16[4,32,1024]{2,1,0:T(8,128)(2,1)}, bf16[4,32,1024]{2,1,0:T(8,128)(2,1)S(1)}, u32[]{:S(2)}, u32[]{:S(2)}) collective-permute-start(bf16[4,32,1024]{2,1,0:T(8,128)(2,1)} %get-tuple-element.36), channel_id=1, source_target_pairs={{0,192},{64,0},{128,64},{192,128},{1,193},{65,1},{129,65},{193,129... | collective-permute-start | bytes 786440 | tf_op jit(solution)/shard_map/ppermute | solution.py:23
  52.2 15.3 %collective-permute-start.13 = (bf16[4,32,1024]{2,1,0:T(8,128)(2,1)S(1)}, bf16[4,32,1024]{2,1,0:T(8,128)(2,1)S(1)}, u32[]{:S(2)}, u32[]{:S(2)}) collective-permute-start(bf16[4,32,1024]{2,1,0:T(8,128)(2,1)S(1)} %get-tuple-element.38), channel_id=1, source_target_pairs={{0,64},{64,128},{128,192},{192,0},{1,65},{65,129},{129,193},{193,1... | collective-permute-start | bytes 786440 | tf_op jit(solution)/shard_map/ppermute | solution.py:23
  69.9 22.6 %collective-permute-start.16 = (bf16[16,2,32,256]{3,2,1,0:T(8,128)(2,1)S(1)}, bf16[16,2,32,256]{3,2,1,0:T(8,128)(2,1)S(1)}, u32[]{:S(2)}, u32[]{:S(2)}) collective-permute-start(bf16[16,2,32,256]{3,2,1,0:T(8,128)(2,1)S(1)} %get-tuple-element.21), channel_id=1, source_target_pairs={{0,0},{1,64},{64,1},{65,65},{128,128},{129,192},{192,129},{193,193... | collective-permute-start | bytes 1572872 | tf_op jit(solution)/shard_map/ppermute | solution.py:213
  75.5 19.9 %collective-permute-start.17 = (bf16[16,2,32,256]{3,2,1,0:T(8,128)(2,1)S(1)}, bf16[16,2,32,256]{3,2,1,0:T(8,128)(2,1)S(1)}, u32[]{:S(2)}, u32[]{:S(2)}) collective-permute-start(bf16[16,2,32,256]{3,2,1,0:T(8,128)(2,1)S(1)} %get-tuple-element.22), channel_id=1, source_target_pairs={{0,64},{1,0},{64,65},{65,1},{128,192},{129,128},{192,193},{193,129... | collective-permute-start | bytes 1572872 | tf_op jit(solution)/shard_map/ppermute | solution.py:213
  96.5 38.7 %all-to-all-start = ((bf16[32,64,256]{2,1,0:T(8,128)(2,1)}), bf16[32,64,256]{2,1,0:T(8,128)(2,1)S(1)}, u32[]{:S(2)}, u32[]{:S(2)}) async-start(bf16[32,64,256]{2,1,0:T(8,128)(2,1)} %bitcast.30), calls=%async_computation | async-start | bytes 2097152 | tf_op jit(solution)/shard_map/all_to_all | solution.py:215
  107.0 81.2 %all-gather.5.cloned.1.call-start = ((), (), s32[]{:S(2)}) async-start(), calls=%async_computation.4 | async-start | bytes 4456448 | tf_op jit(solution)/shard_map/all_gather | solution.py:176
  180.1 19.9 %all-to-all-start.2 = ((bf16[16,128,256]{2,1,0:T(8,128)(2,1)}), bf16[16,128,256]{2,1,0:T(8,128)(2,1)S(1)}, u32[]{:S(2)}, u32[]{:S(2)}) async-start(bf16[16,128,256]{2,1,0:T(8,128)(2,1)} %bitcast.37), calls=%async_computation.2 | async-start | bytes 2097152 | tf_op jit(solution)/shard_map/all_to_all | solution.py:230
  200.0 2.2 %copy-start = (bf16[2048,1024]{1,0:T(8,128)(2,1)S(1)}, bf16[2048,1024]{1,0:T(8,128)(2,1)}, u32[]{:S(2)}) copy-start(bf16[2048,1024]{1,0:T(8,128)(2,1)} %all-gather.5.cloned.1.call-done) | copy-start | bytes 12582916
Sparse Core Ops, SparseCore 0:
  31.6 92.9 all-gather.2
  135.3 52.8 all-gather.4

commit v4 on v3

--- a/solution.py
+++ b/solution.py
@@ -104,12 +104,11 @@
     first_out[...] = first_new
     second_out[...] = second_new
     direction = first_new / bias_one / (jnp.sqrt(second_new / bias_two) + epsilon)
-    turned = lax.dot_general(
-        direction.astype(jnp.bfloat16).T,
-        left,
-        (((1,), (1,)), ((), ())),
-        preferred_element_type=jnp.float32,
-    ).astype(jnp.bfloat16)
+    turned = (
+        jnp.dot(left, direction.astype(jnp.bfloat16), preferred_element_type=jnp.float32)
+        .astype(jnp.bfloat16)
+        .T
+    )
     for z in range(4):
         back[4 * z : 4 * z + 4, 0] = turned[:, z * ROWS : (z + 1) * ROWS].reshape(4, 32, ROWS)
 
@@ -191,7 +190,12 @@
     kept = for_x(0, halves)
     given = lax.ppermute(for_x(2, halves), "x", [(i, i ^ 2) for i in range(4)])
 
-    line = line_gather(jnp.concatenate([right_basis, left_basis]), zl)
+    both = jnp.where(
+        lax.broadcasted_iota(jnp.int32, (6, 16, BLOCK), 0) < 2,
+        jnp.pad(right_basis, ((0, 4), (0, 0), (0, 0))),
+        jnp.pad(left_basis, ((2, 0), (0, 0), (0, 0))),
+    )
+    line = line_gather(both, zl)
     given, line = tie((given, line))
     left_whole = gather_whole(line[2:])
     right = line[0], line[1]
@@ -211,14 +215,14 @@
             for c in range(2)
         ]
         moved.append(lax.ppermute(sent[t], ("x", "core"), pairs))
+    moved, right_line = tie((moved, line[:2]))
     moved = jnp.stack(moved, axis=2).reshape(32, 64, ROWS)
     owned = lax.all_to_all(moved, ("y", "zl", "zh"), split_axis=0, concat_axis=0, tiled=True)
     owned = owned.reshape(4, 16, 32, ROWS)
-    owned, right_line = tie((owned, line[:2]))
     right_whole = gather_whole(right_line)
-    left_whole, first_moment, second_moment = (
+    left_whole, right_whole, first_moment, second_moment = (
         pltpu.with_memory_space_constraint(value, pltpu.HBM)
-        for value in (left_whole, first_moment, second_moment)
+        for value in (left_whole, right_whole, first_moment, second_moment)
     )
     back, first_new, second_new = middle_stage(
         place, owned, left_whole, first_moment, second_moment

time: 214 us -> 211 us (0.986)
  blocking collectives: 33.2 us -> 71.3 us
  waiting for transfers between devices: 91.3 us -> 64.2 us
  starting transfers between devices: 45.8 us -> 35.9 us
  local copies, waits for them, and re-layouts: 8.84 us -> 3.83 us
    all_to_all x0 -> x1, blocking collectives: none -> 36.4 us  [on_device(): lax.all_to_all(moved, ('y', 'zl', 'zh'), split_axis=0, concat_axis=0, til...]
    all_to_all x1 -> x0, waiting for transfers between devices: 26.4 us -> none  [on_device(): lax.all_to_all(moved, ('y', 'zl', 'zh'), split_axis=0, concat_axis=0, til...]
    all_to_all x1 -> x0, starting transfers between devices: 10.5 us -> none  [on_device(): lax.all_to_all(moved, ('y', 'zl', 'zh'), split_axis=0, concat_axis=0, til...]
    unnamed x5 -> x2, local copies, waits for them, and re-layouts: 3.04 us -> 0.01 us
  transfers between devices with their start and end apart: 22 -> 21, of which waited for: 11 -> 12; matrix products, arithmetic and copies ran while one was open for 3% -> 3% of each run, Pallas kernels for 6% -> 6%
where the time goes in v4:
time: 211 us; the launch traced here: 210 us
  blocking collectives  71.3 us (34%)
  waiting for transfers between devices  64.2 us (30%)
  starting transfers between devices  35.9 us (17%)
  Pallas kernels  17.3 us (8%)
  between operations  14.2 us (7%)
  local copies, waits for them, and re-layouts  3.83 us (2%)
  other arithmetic  3.55 us (2%)
    all_to_all x1, blocking collectives, on_device(): lax.all_to_all(moved, ('y', 'zl', 'zh'), split_axis=0, concat_axis=0, til...  36.4 us
    all_to_all x1, blocking collectives, on_device(): lax.all_to_all(back.reshape(16, 128, ROWS), ZC, split_axis=0, concat_axis...  34.9 us
    ppermute x15, waiting for transfers between devices, shift(): return lax.ppermute(value, axis, [(i, (i + by) % 4) for i in range(4)])  27.8 us
    ppermute x15, starting transfers between devices, shift(): return lax.ppermute(value, axis, [(i, (i + by) % 4) for i in range(4)])  22.8 us
    ppermute x2, waiting for transfers between devices, on_device(): moved.append(lax.ppermute(sent[t], ('x', 'core'), pairs))  18.8 us
    all_to_all x1, waiting for transfers between devices, on_device(): back = lax.all_to_all(back, XY, split_axis=0, concat_axis=0, tiled=True)  13.4 us
    pallas_call x1, Pallas kernels, middle_stage(): pl.pallas_call(middle_kernel, out_shape=(jax.ShapeDtypeStruct((16, 4, 32,...  9.87 us
    ppermute x2, starting transfers between devices, on_device(): moved.append(lax.ppermute(sent[t], ('x', 'core'), pairs))  5.86 us
  transfers between devices with their start and end apart: 21, of which 12 were waited for; matrix products, arithmetic and copies ran while one was open for 3% of the time, Pallas kernels for 6%

profile of v4, /device:TPU:1, one launch (start us, length us, event | category | flops | bytes accessed | tf_op | source)
XLA Modules:
  0.0 210.3 jit_solution(4466753606123818965)
XLA Ops:
  8.2 2.5 %collective-permute-start.1 = (bf16[6,16,1024]{2,1,0:T(8,128)(2,1)S(1)}, bf16[6,16,1024]{2,1,0:T(8,128)(2,1)S(1)}, u32[]{:S(2)}, u32[]{:S(2)}) collective-permute-start(bf16[6,16,1024]{2,1,0:T(8,128)(2,1)S(1)} %pad_select_fusion), channel_id=1, source_target_pairs={{0,4},{4,8},{8,12},{12,0},{1,5},{5,9},{9,13},{13,1},{2,6},{6,10},{... | collective-permute-start | bytes 589832 | tf_op jit(solution)/shard_map/ppermute | solution.py:23
  10.8 3.0 %collective-permute-start.2 = (bf16[6,16,1024]{2,1,0:T(8,128)(2,1)S(1)}, bf16[6,16,1024]{2,1,0:T(8,128)(2,1)S(1)}, u32[]{:S(2)}, u32[]{:S(2)}) collective-permute-start(bf16[6,16,1024]{2,1,0:T(8,128)(2,1)S(1)} %pad_select_fusion), channel_id=1, source_target_pairs={{0,8},{4,12},{8,0},{12,4},{1,9},{5,13},{9,1},{13,5},{2,10},{6,14},... | collective-permute-start | bytes 589832 | tf_op jit(solution)/shard_map/ppermute | solution.py:23
  14.5 1.3 broadcast_select_fusion
  15.8 2.8 %collective-permute-start = (bf16[256,1024]{1,0:T(8,128)(2,1)S(1)}, bf16[256,1024]{1,0:T(8,128)(2,1)S(1)}, u32[]{:S(2)}, u32[]{:S(2)}) collective-permute-start(bf16[256,1024]{1,0:T(8,128)(2,1)S(1)} %get-tuple-element.25), channel_id=1, source_target_pairs={{0,128},{64,192},{128,0},{192,64},{1,129},{65,193},{129,1},{193,65... | collective-permute-start | bytes 1572872 | tf_op jit(solution)/shard_map/ppermute | solution.py:191
  18.6 8.7 %collective-permute-done.2 = bf16[6,16,1024]{2,1,0:T(8,128)(2,1)S(1)} collective-permute-done((bf16[6,16,1024]{2,1,0:T(8,128)(2,1)S(1)}, bf16[6,16,1024]{2,1,0:T(8,128)(2,1)S(1)}, u32[]{:S(2)}, u32[]{:S(2)}) %collective-permute-start.2) | collective-permute-done | bytes 196640 | tf_op jit(solution)/shard_map/ppermute | solution.py:23
  27.6 1.7 collective-permute-done.given
  30.2 1.3 collective-permute-start.4
  31.5 1.5 collective-permute-start.5
  32.9 1.5 collective-permute-start.6
  34.5 1.4 collective-permute-start.7
  35.9 1.5 collective-permute-start.8
  37.4 1.6 collective-permute-start.9
  39.7 3.1 %collective-permute-done.9 = bf16[2,32,1024]{2,1,0:T(8,128)(2,1)S(1)} collective-permute-done((bf16[2,32,1024]{2,1,0:T(8,128)(2,1)S(1)}, bf16[2,32,1024]{2,1,0:T(8,128)(2,1)S(1)}, u32[]{:S(2)}, u32[]{:S(2)}) %collective-permute-start.9) | collective-permute-done | bytes 131104 | tf_op jit(solution)/shard_map/ppermute | solution.py:23
  44.0 2.4 %collective-permute-start.14 = (bf16[4,32,1024]{2,1,0:T(8,128)(2,1)}, bf16[4,32,1024]{2,1,0:T(8,128)(2,1)S(1)}, u32[]{:S(2)}, u32[]{:S(2)}) collective-permute-start(bf16[4,32,1024]{2,1,0:T(8,128)(2,1)} %get-tuple-element.38), channel_id=1, source_target_pairs={{0,192},{64,0},{128,64},{192,128},{1,193},{65,1},{129,65},{193,129... | collective-permute-start | bytes 786440 | tf_op jit(solution)/shard_map/ppermute | solution.py:23
  46.9 2.4 %collective-permute-start.11 = (bf16[4,32,1024]{2,1,0:T(8,128)(2,1)S(1)}, bf16[4,32,1024]{2,1,0:T(8,128)(2,1)S(1)}, u32[]{:S(2)}, u32[]{:S(2)}) collective-permute-start(bf16[4,32,1024]{2,1,0:T(8,128)(2,1)S(1)} %pad_maximum_fusion.3.refs_0_), channel_id=1, source_target_pairs={{0,48},{16,0},{32,16},{48,32},{1,49},{17,1},{33,17},{49,33},{2,50}... | collective-permute-start | bytes 786440 | tf_op jit(solution)/shard_map/ppermute | solution.py:23
  50.1 2.2 %collective-permute-start.12 = (bf16[4,32,1024]{2,1,0:T(8,128)(2,1)S(1)}, bf16[4,32,1024]{2,1,0:T(8,128)(2,1)S(1)}, u32[]{:S(2)}, u32[]{:S(2)}) collective-permute-start(bf16[4,32,1024]{2,1,0:T(8,128)(2,1)S(1)} %pad_maximum_fusion.3.refs_0_), channel_id=1, source_target_pairs={{0,32},{16,48},{32,0},{48,16},{1,33},{17,49},{33,1},{49,17},{2,34}... | collective-permute-start | bytes 786440 | tf_op jit(solution)/shard_map/ppermute | solution.py:23
  52.4 5.6 %collective-permute-done.14.refs_6_ = bf16[4,32,1024]{2,1,0:T(8,128)(2,1)S(1)} collective-permute-done((bf16[4,32,1024]{2,1,0:T(8,128)(2,1)}, bf16[4,32,1024]{2,1,0:T(8,128)(2,1)S(1)}, u32[]{:S(2)}, u32[]{:S(2)}) %collective-permute-start.14) | collective-permute-done | bytes 262176 | tf_op jit(solution)/shard_map/ppermute | solution.py:23
  58.0 2.9 %collective-permute-done.15.refs_7_ = bf16[4,32,1024]{2,1,0:T(8,128)(2,1)S(1)} collective-permute-done((bf16[4,32,1024]{2,1,0:T(8,128)(2,1)S(1)}, bf16[4,32,1024]{2,1,0:T(8,128)(2,1)S(1)}, u32[]{:S(2)}, u32[]{:S(2)}) %collective-permute-start.15) | collective-permute-done | bytes 262176 | tf_op jit(solution)/shard_map/ppermute | solution.py:23
  61.0 5.9 %collective-permute-done.12.refs_3_ = bf16[4,32,1024]{2,1,0:T(8,128)(2,1)S(1)} collective-permute-done((bf16[4,32,1024]{2,1,0:T(8,128)(2,1)S(1)}, bf16[4,32,1024]{2,1,0:T(8,128)(2,1)S(1)}, u32[]{:S(2)}, u32[]{:S(2)}) %collective-permute-start.12) | collective-permute-done | bytes 262176 | tf_op jit(solution)/shard_map/ppermute | solution.py:23
  66.9 2.4 %rotate_columns.1 = bf16[2,16,2,32,256]{4,3,2,1,0:T(8,128)(2,1)S(1)} custom-call(s32[4]{0:T(128)S(1)} %pad_add_fusion.place, bf16[256,1024]{1,0:T(8,128)(2,1)S(1)} %get-tuple-element.26.kept, bf16[256,1024]{1,0:T(8,128)(2,1)S(1)} %collective-permute-done.given, bf16[4,32,1024]{2,1,0:T(8,128)(2,1)S(1)} %pad_maximum_fusion.3.refs_0_, ...), custom_call_target="tpu_custom_call" | custom-call | flops 1073741824 | bytes 4194304 | tf_op jit(solution)/shard_map/rotate_columns/pallas_call | solution.py:68
  69.4 5.8 %collective-permute-start.16 = (bf16[16,2,32,256]{3,2,1,0:T(8,128)(2,1)S(1)}, bf16[16,2,32,256]{3,2,1,0:T(8,128)(2,1)S(1)}, u32[]{:S(2)}, u32[]{:S(2)}) collective-permute-start(bf16[16,2,32,256]{3,2,1,0:T(8,128)(2,1)S(1)} %get-tuple-element.24), channel_id=1, source_target_pairs={{0,0},{1,64},{64,1},{65,65},{128,128},{129,192},{192,129},{193,193... | collective-permute-start | bytes 1572872 | tf_op jit(solution)/shard_map/ppermute | solution.py:217
  75.3 1.7 slice.63
  77.0 16.0 %collective-permute-done.16 = bf16[16,2,32,256]{3,2,1,0:T(8,128)(2,1)S(1)} collective-permute-done((bf16[16,2,32,256]{3,2,1,0:T(8,128)(2,1)S(1)}, bf16[16,2,32,256]{3,2,1,0:T(8,128)(2,1)S(1)}, u32[]{:S(2)}, u32[]{:S(2)}) %collective-permute-start.16) | collective-permute-done | bytes 524320 | tf_op jit(solution)/shard_map/ppermute | solution.py:217
  93.0 2.8 %collective-permute-done.17 = bf16[16,2,32,256]{3,2,1,0:T(8,128)(2,1)S(1)} collective-permute-done((bf16[16,2,32,256]{3,2,1,0:T(8,128)(2,1)S(1)}, bf16[16,2,32,256]{3,2,1,0:T(8,128)(2,1)S(1)}, u32[]{:S(2)}, u32[]{:S(2)}) %collective-permute-start.17) | collective-permute-done | bytes 524320 | tf_op jit(solution)/shard_map/ppermute | solution.py:217
  96.0 36.4 %all_to_all.15 = bf16[32,64,256]{2,1,0:T(8,128)(2,1)S(1)} all-to-all(bf16[32,64,256]{2,1,0:T(8,128)(2,1)S(1)} %bitcast.66), channel_id=1, replica_groups=mesh['x'=4,'y'=4,'zl'=4,'zh'=2,'core'=2] {'y','zl','zh'}, dimensions={0} | all-to-all | bytes 2097152 | tf_op jit(solution)/shard_map/all_to_all | solution.py:220
  132.4 9.9 %moments_and_direction.1 = (bf16[16,4,32,256]{3,2,1,0:T(8,128)(2,1)S(1)}, f32[4096,128]{1,0:T(8,128)}, f32[4096,128]{1,0:T(8,128)}) custom-call(s32[4]{0:T(128)S(1)} %pad_add_fusion.place, bf16[4,16,32,256]{3,2,1,0:T(8,128)(2,1)S(1)} %bitcast.58, bf16[16,4,64,1024]{3,2,1,0:T(8,128)(2,1)} %bitcast.60, f32[4096,128]{1,0:T(8,128)} %first.1, f32[4096,128]{1,0:T(8,128)} %second.1), custom_call_target="tpu_custom_call" | custom-call | flops 2147483648 | bytes 18874368 | tf_op jit(solution)/shard_map/moments_and_direction/pallas_call | solution.py:119
  142.3 34.9 %all_to_all.16 = bf16[16,128,256]{2,1,0:T(8,128)(2,1)S(1)} all-to-all(bf16[16,128,256]{2,1,0:T(8,128)(2,1)S(1)} %bitcast.59), channel_id=1, replica_groups=mesh['x'=4,'y'=4,'zl'=4,'zh'=2,'core'=2] {'zl','zh','core'}, dimensions={0} | all-to-all | bytes 2097152 | tf_op jit(solution)/shard_map/all_to_all | solution.py:230
  177.2 1.1 copy.17
  178.3 4.3 %all-to-all-start.2 = ((bf16[16,128,256]{2,1,0:T(8,128)(2,1)}), bf16[16,128,256]{2,1,0:T(8,128)(2,1)S(1)}, u32[]{:S(2)}, u32[]{:S(2)}) async-start(bf16[16,128,256]{2,1,0:T(8,128)(2,1)} %bitcast.37), calls=%async_computation.2 | async-start | bytes 2097152 | tf_op jit(solution)/shard_map/all_to_all | solution.py:234
  182.6 2.4 %all-gather.5.cloned.1.call-done = bf16[2048,1024]{1,0:T(8,128)(2,1)} async-done(((bf16[128,1024]{1,0:T(8,128)(2,1)}), bf16[2048,1024]{1,0:T(8,128)(2,1)}) %all-gather.5.cloned.1.call-update) | async-done | bytes 4194320 | tf_op jit(solution)/shard_map/all_gather | solution.py:175
  185.0 13.4 %all-to-all-done.2.back = bf16[16,128,256]{2,1,0:T(8,128)(2,1)S(1)} async-done(((bf16[16,128,256]{2,1,0:T(8,128)(2,1)}), bf16[16,128,256]{2,1,0:T(8,128)(2,1)S(1)}, u32[]{:S(2)}, u32[]{:S(2)}) %all-to-all-start.2) | async-done | bytes 1048608 | tf_op jit(solution)/shard_map/all_to_all | solution.py:234
  198.4 5.1 %rotate_back_columns.1 = f32[256,2048]{1,0:T(8,128)} custom-call(bf16[16,128,256]{2,1,0:T(8,128)(2,1)S(1)} %all-to-all-done.2.back, bf16[16,2,64,1024]{3,2,1,0:T(8,128)(2,1)} %bitcast.65), custom_call_target="tpu_custom_call" | custom-call | flops 1073741824 | bytes 7340032 | tf_op jit(solution)/shard_map/rotate_back_columns/pallas_call | solution.py:157
  (37 shorter events, 6.7 us)
Async XLA Ops:
  7.2 125.2 %all-gather.3.cloned.1.call-start = ((), (), s32[]{:S(2)}) async-start(), calls=%async_computation.3 | async-start | bytes 8912896 | tf_op jit(solution)/shard_map/all_gather | solution.py:175
  8.2 10.4 %collective-permute-start.1 = (bf16[6,16,1024]{2,1,0:T(8,128)(2,1)S(1)}, bf16[6,16,1024]{2,1,0:T(8,128)(2,1)S(1)}, u32[]{:S(2)}, u32[]{:S(2)}) collective-permute-start(bf16[6,16,1024]{2,1,0:T(8,128)(2,1)S(1)} %pad_select_fusion), channel_id=1, source_target_pairs={{0,4},{4,8},{8,12},{12,0},{1,5},{5,9},{9,13},{13,1},{2,6},{6,10},{... | collective-permute-start | bytes 589832 | tf_op jit(solution)/shard_map/ppermute | solution.py:23
  10.8 16.5 %collective-permute-start.2 = (bf16[6,16,1024]{2,1,0:T(8,128)(2,1)S(1)}, bf16[6,16,1024]{2,1,0:T(8,128)(2,1)S(1)}, u32[]{:S(2)}, u32[]{:S(2)}) collective-permute-start(bf16[6,16,1024]{2,1,0:T(8,128)(2,1)S(1)} %pad_select_fusion), channel_id=1, source_target_pairs={{0,8},{4,12},{8,0},{12,4},{1,9},{5,13},{9,1},{13,5},{2,10},{6,14},... | collective-permute-start | bytes 589832 | tf_op jit(solution)/shard_map/ppermute | solution.py:23
  13.8 13.5 %collective-permute-start.3 = (bf16[6,16,1024]{2,1,0:T(8,128)(2,1)S(1)}, bf16[6,16,1024]{2,1,0:T(8,128)(2,1)S(1)}, u32[]{:S(2)}, u32[]{:S(2)}) collective-permute-start(bf16[6,16,1024]{2,1,0:T(8,128)(2,1)S(1)} %pad_select_fusion), channel_id=1, source_target_pairs={{0,12},{4,0},{8,4},{12,8},{1,13},{5,1},{9,5},{13,9},{2,14},{6,2},{... | collective-permute-start | bytes 589832 | tf_op jit(solution)/shard_map/ppermute | solution.py:23
  15.8 13.5 %collective-permute-start = (bf16[256,1024]{1,0:T(8,128)(2,1)S(1)}, bf16[256,1024]{1,0:T(8,128)(2,1)S(1)}, u32[]{:S(2)}, u32[]{:S(2)}) collective-permute-start(bf16[256,1024]{1,0:T(8,128)(2,1)S(1)} %get-tuple-element.25), channel_id=1, source_target_pairs={{0,128},{64,192},{128,0},{192,64},{1,129},{65,193},{129,1},{193,65... | collective-permute-start | bytes 1572872 | tf_op jit(solution)/shard_map/ppermute | solution.py:191
  27.5 16.1 %copy-start = (bf16[6,4,16,1024]{3,2,1,0:T(8,128)(2,1)}, bf16[6,4,16,1024]{3,2,1,0:T(8,128)(2,1)S(1)}, u32[]{:S(2)}) copy-start(bf16[6,4,16,1024]{3,2,1,0:T(8,128)(2,1)S(1)} %copy.12) | copy-start | bytes 2359300
  30.1 154.9 %all-gather.5.cloned.1.call-start = ((), (), s32[]{:S(2)}) async-start(), calls=%async_computation.4 | async-start | bytes 4456448 | tf_op jit(solution)/shard_map/all_gather | solution.py:175
  30.2 7.2 %collective-permute-start.4 = (bf16[32,1024]{1,0:T(8,128)(2,1)S(1)}, bf16[32,1024]{1,0:T(8,128)(2,1)S(1)}, u32[]{:S(2)}, u32[]{:S(2)}) collective-permute-start(bf16[32,1024]{1,0:T(8,128)(2,1)S(1)} %get-tuple-element.32), channel_id=1, source_target_pairs={{0,64},{64,128},{128,192},{192,0},{1,65},{65,129},{129,193},{193,1... | collective-permute-start | bytes 196616 | tf_op jit(solution)/shard_map/ppermute | solution.py:23
  31.5 7.5 %collective-permute-start.5 = (bf16[32,1024]{1,0:T(8,128)(2,1)S(1)}, bf16[32,1024]{1,0:T(8,128)(2,1)S(1)}, u32[]{:S(2)}, u32[]{:S(2)}) collective-permute-start(bf16[32,1024]{1,0:T(8,128)(2,1)S(1)} %get-tuple-element.30), channel_id=1, source_target_pairs={{0,192},{64,0},{128,64},{192,128},{1,193},{65,1},{129,65},{193,129... | collective-permute-start | bytes 196616 | tf_op jit(solution)/shard_map/ppermute | solution.py:23
  32.9 6.0 %collective-permute-start.6 = (bf16[32,1024]{1,0:T(8,128)(2,1)S(1)}, bf16[32,1024]{1,0:T(8,128)(2,1)S(1)}, u32[]{:S(2)}, u32[]{:S(2)}) collective-permute-start(bf16[32,1024]{1,0:T(8,128)(2,1)S(1)} %get-tuple-element.31), channel_id=1, source_target_pairs={{0,128},{64,192},{128,0},{192,64},{1,129},{65,193},{129,1},{193,65... | collective-permute-start | bytes 196616 | tf_op jit(solution)/shard_map/ppermute | solution.py:23
  34.5 5.2 %collective-permute-start.7 = (bf16[2,32,1024]{2,1,0:T(8,128)(2,1)S(1)}, bf16[2,32,1024]{2,1,0:T(8,128)(2,1)S(1)}, u32[]{:S(2)}, u32[]{:S(2)}) collective-permute-start(bf16[2,32,1024]{2,1,0:T(8,128)(2,1)S(1)} %get-tuple-element.28), channel_id=1, source_target_pairs={{0,16},{16,32},{32,48},{48,0},{1,17},{17,33},{33,49},{49,1},{2,18}... | collective-permute-start | bytes 393224 | tf_op jit(solution)/shard_map/ppermute | solution.py:23
  35.9 3.8 %collective-permute-start.8 = (bf16[2,32,1024]{2,1,0:T(8,128)(2,1)S(1)}, bf16[2,32,1024]{2,1,0:T(8,128)(2,1)S(1)}, u32[]{:S(2)}, u32[]{:S(2)}) collective-permute-start(bf16[2,32,1024]{2,1,0:T(8,128)(2,1)S(1)} %get-tuple-element.28), channel_id=1, source_target_pairs={{0,48},{16,0},{32,16},{48,32},{1,49},{17,1},{33,17},{49,33},{2,50}... | collective-permute-start | bytes 393224 | tf_op jit(solution)/shard_map/ppermute | solution.py:23
  37.4 5.4 %collective-permute-start.9 = (bf16[2,32,1024]{2,1,0:T(8,128)(2,1)S(1)}, bf16[2,32,1024]{2,1,0:T(8,128)(2,1)S(1)}, u32[]{:S(2)}, u32[]{:S(2)}) collective-permute-start(bf16[2,32,1024]{2,1,0:T(8,128)(2,1)S(1)} %get-tuple-element.28), channel_id=1, source_target_pairs={{0,32},{16,48},{32,0},{48,16},{1,33},{17,49},{33,1},{49,17},{2,34}... | collective-permute-start | bytes 393224 | tf_op jit(solution)/shard_map/ppermute | solution.py:23
  43.7 6.5 %collective-permute-start.13 = (bf16[4,32,1024]{2,1,0:T(8,128)(2,1)S(1)}, bf16[4,32,1024]{2,1,0:T(8,128)(2,1)S(1)}, u32[]{:S(2)}, u32[]{:S(2)}) collective-permute-start(bf16[4,32,1024]{2,1,0:T(8,128)(2,1)S(1)} %get-tuple-element.40), channel_id=1, source_target_pairs={{0,64},{64,128},{128,192},{192,0},{1,65},{65,129},{129,193},{193,1... | collective-permute-start | bytes 786440 | tf_op jit(solution)/shard_map/ppermute | solution.py:23
  44.0 14.1 %collective-permute-start.14 = (bf16[4,32,1024]{2,1,0:T(8,128)(2,1)}, bf16[4,32,1024]{2,1,0:T(8,128)(2,1)S(1)}, u32[]{:S(2)}, u32[]{:S(2)}) collective-permute-start(bf16[4,32,1024]{2,1,0:T(8,128)(2,1)} %get-tuple-element.38), channel_id=1, source_target_pairs={{0,192},{64,0},{128,64},{192,128},{1,193},{65,1},{129,65},{193,129... | collective-permute-start | bytes 786440 | tf_op jit(solution)/shard_map/ppermute | solution.py:23
  46.3 14.6 %collective-permute-start.15 = (bf16[4,32,1024]{2,1,0:T(8,128)(2,1)S(1)}, bf16[4,32,1024]{2,1,0:T(8,128)(2,1)S(1)}, u32[]{:S(2)}, u32[]{:S(2)}) collective-permute-start(bf16[4,32,1024]{2,1,0:T(8,128)(2,1)S(1)} %get-tuple-element.37), channel_id=1, source_target_pairs={{0,128},{64,192},{128,0},{192,64},{1,129},{65,193},{129,1},{193,65... | collective-permute-start | bytes 786440 | tf_op jit(solution)/shard_map/ppermute | solution.py:23
  46.6 14.4 %collective-permute-start.10 = (bf16[4,32,1024]{2,1,0:T(8,128)(2,1)S(1)}, bf16[4,32,1024]{2,1,0:T(8,128)(2,1)S(1)}, u32[]{:S(2)}, u32[]{:S(2)}) collective-permute-start(bf16[4,32,1024]{2,1,0:T(8,128)(2,1)S(1)} %pad_maximum_fusion.3.refs_0_), channel_id=1, source_target_pairs={{0,16},{16,32},{32,48},{48,0},{1,17},{17,33},{33,49},{49,1},{2,18}... | collective-permute-start | bytes 786440 | tf_op jit(solution)/shard_map/ppermute | solution.py:23
  46.9 14.1 %collective-permute-start.11 = (bf16[4,32,1024]{2,1,0:T(8,128)(2,1)S(1)}, bf16[4,32,1024]{2,1,0:T(8,128)(2,1)S(1)}, u32[]{:S(2)}, u32[]{:S(2)}) collective-permute-start(bf16[4,32,1024]{2,1,0:T(8,128)(2,1)S(1)} %pad_maximum_fusion.3.refs_0_), channel_id=1, source_target_pairs={{0,48},{16,0},{32,16},{48,32},{1,49},{17,1},{33,17},{49,33},{2,50}... | collective-permute-start | bytes 786440 | tf_op jit(solution)/shard_map/ppermute | solution.py:23
  50.1 16.8 %collective-permute-start.12 = (bf16[4,32,1024]{2,1,0:T(8,128)(2,1)S(1)}, bf16[4,32,1024]{2,1,0:T(8,128)(2,1)S(1)}, u32[]{:S(2)}, u32[]{:S(2)}) collective-permute-start(bf16[4,32,1024]{2,1,0:T(8,128)(2,1)S(1)} %pad_maximum_fusion.3.refs_0_), channel_id=1, source_target_pairs={{0,32},{16,48},{32,0},{48,16},{1,33},{17,49},{33,1},{49,17},{2,34}... | collective-permute-start | bytes 786440 | tf_op jit(solution)/shard_map/ppermute | solution.py:23
  69.4 23.6 %collective-permute-start.16 = (bf16[16,2,32,256]{3,2,1,0:T(8,128)(2,1)S(1)}, bf16[16,2,32,256]{3,2,1,0:T(8,128)(2,1)S(1)}, u32[]{:S(2)}, u32[]{:S(2)}) collective-permute-start(bf16[16,2,32,256]{3,2,1,0:T(8,128)(2,1)S(1)} %get-tuple-element.24), channel_id=1, source_target_pairs={{0,0},{1,64},{64,1},{65,65},{128,128},{129,192},{192,129},{193,193... | collective-permute-start | bytes 1572872 | tf_op jit(solution)/shard_map/ppermute | solution.py:217
  75.2 20.6 %collective-permute-start.17 = (bf16[16,2,32,256]{3,2,1,0:T(8,128)(2,1)S(1)}, bf16[16,2,32,256]{3,2,1,0:T(8,128)(2,1)S(1)}, u32[]{:S(2)}, u32[]{:S(2)}) collective-permute-start(bf16[16,2,32,256]{3,2,1,0:T(8,128)(2,1)S(1)} %get-tuple-element.23), channel_id=1, source_target_pairs={{0,64},{1,0},{64,65},{65,1},{128,192},{129,128},{192,193},{193,129... | collective-permute-start | bytes 1572872 | tf_op jit(solution)/shard_map/ppermute | solution.py:217
  178.3 20.1 %all-to-all-start.2 = ((bf16[16,128,256]{2,1,0:T(8,128)(2,1)}), bf16[16,128,256]{2,1,0:T(8,128)(2,1)S(1)}, u32[]{:S(2)}, u32[]{:S(2)}) async-start(bf16[16,128,256]{2,1,0:T(8,128)(2,1)} %bitcast.37), calls=%async_computation.2 | async-start | bytes 2097152 | tf_op jit(solution)/shard_map/all_to_all | solution.py:234
Sparse Core Ops, SparseCore 0:
  30.2 93.0 all-gather.2
  125.7 59.1 all-gather.4

commit v5 on v4

--- a/solution.py
+++ b/solution.py
@@ -12,7 +12,7 @@
 epsilon = 1e-08
 
 XY = ("x", "y")
-ZC = ("zl", "zh", "core")
+ZC = ("zh", "core", "zl")
 NEAR = (0, -1, 1, 2)
 BLOCK = 1024
 ROWS = 256
@@ -61,20 +61,20 @@
     turned = jnp.dot(rows, whole[...], preferred_element_type=jnp.float32)
     turned = turned.astype(jnp.bfloat16).T
     for low in range(2):
-        sent[low ^ core, :, 0] = turned[512 * low : 512 * low + 512].reshape(16, 32, ROWS)
+        sent[low ^ core, 0] = turned[512 * low : 512 * low + 512].reshape(16, 32, ROWS)
 
 
 def first_stage(place, kept, given, pieces):
     return pl.pallas_call(
         first_kernel,
-        out_shape=jax.ShapeDtypeStruct((2, 16, 2, 32, ROWS), jnp.bfloat16),
+        out_shape=jax.ShapeDtypeStruct((2, 2, 16, 32, ROWS), jnp.bfloat16),
         grid_spec=pltpu.PrefetchScalarGridSpec(
             num_scalar_prefetch=1,
             grid=(2,),
             in_specs=[pl.BlockSpec((ROWS, BLOCK), lambda g, place: (0, 0))] * 2
             + [pl.BlockSpec((4, 32, BLOCK), lambda g, place: (0, 0, 0))] * len(pieces),
             out_specs=pl.BlockSpec(
-                (2, 16, 1, 32, ROWS), lambda g, place: (0, 0, (place[0] >> 1) ^ g, 0, 0)
+                (2, 1, 16, 32, ROWS), lambda g, place: (0, (place[0] >> 1) ^ g, 0, 0, 0)
             ),
             scratch_shapes=[pltpu.VMEM((BLOCK, BLOCK), jnp.bfloat16)],
         ),
@@ -92,7 +92,7 @@
     columns = jnp.concatenate(
         [
             jnp.concatenate(
-                [owned[0, 4 * z + (q & 2) + ((q & 1) ^ low)] for q in range(4)], axis=0
+                [owned[q >> 1, 0, 2 * z + ((q & 1) ^ low)] for q in range(4)], axis=0
             )
             for z in range(4)
         ],
@@ -110,7 +110,8 @@
         .T
     )
     for z in range(4):
-        back[4 * z : 4 * z + 4, 0] = turned[:, z * ROWS : (z + 1) * ROWS].reshape(4, 32, ROWS)
+        for q in range(4):
+            back[4 * q + z, 0] = turned[32 * q : 32 * q + 32, z * ROWS : (z + 1) * ROWS]
 
 
 def middle_stage(place, owned, left_whole, first_moment, second_moment):
@@ -127,7 +128,7 @@
             num_scalar_prefetch=1,
             grid=(4,),
             in_specs=[
-                pl.BlockSpec((1, 16, 32, ROWS), lambda b, place: (b, 0, 0, 0)),
+                pl.BlockSpec((2, 1, 8, 32, ROWS), lambda b, place: (0, b, 0, 0, 0)),
                 pl.BlockSpec((16, 1, 64, BLOCK), lambda b, place: (0, b, 0, 0)),
                 moments,
                 moments,
@@ -146,7 +147,7 @@
 
 def last_kernel(back, right_whole, update):
     update[...] = lax.dot_general(
-        back[...].reshape(BLOCK, ROWS).T,
+        jnp.concatenate([back[y, x] for x in range(2) for y in range(4)], axis=0).T,
         right_whole[:, 0].reshape(BLOCK // 2, BLOCK),
         (((1,), (1,)), ((), ())),
         preferred_element_type=jnp.float32,
@@ -159,7 +160,7 @@
         out_shape=jax.ShapeDtypeStruct((ROWS, 2 * BLOCK), jnp.float32),
         grid=(2, 2),
         in_specs=[
-            pl.BlockSpec((8, 128, ROWS), lambda k, i: (k, 0, 0)),
+            pl.BlockSpec((4, 2, 128, ROWS), lambda k, i: (0, k, 0, 0)),
             pl.BlockSpec((8, 1, 64, BLOCK), lambda k, i: (i, k, 0, 0)),
         ],
         out_specs=pl.BlockSpec((ROWS, BLOCK // 2), lambda k, i: (0, 2 * k + i)),
@@ -217,8 +218,8 @@
         moved.append(lax.ppermute(sent[t], ("x", "core"), pairs))
     moved, right_line = tie((moved, line[:2]))
     moved = jnp.stack(moved, axis=2).reshape(32, 64, ROWS)
-    owned = lax.all_to_all(moved, ("y", "zl", "zh"), split_axis=0, concat_axis=0, tiled=True)
-    owned = owned.reshape(4, 16, 32, ROWS)
+    owned = lax.all_to_all(moved, ("zh", "y", "zl"), split_axis=0, concat_axis=0, tiled=True)
+    owned = owned.reshape(2, 4, 8, 32, ROWS)
     right_whole = gather_whole(right_line)
     left_whole, right_whole, first_moment, second_moment = (
         pltpu.with_memory_space_constraint(value, pltpu.HBM)
@@ -230,8 +231,9 @@
     back = lax.all_to_all(
         back.reshape(16, 128, ROWS), ZC, split_axis=0, concat_axis=0, tiled=True
     )
-    back = back.reshape(4, 4, 4, 32, ROWS).transpose(1, 2, 0, 3, 4).reshape(16, 128, ROWS)
-    back = lax.all_to_all(back, XY, split_axis=0, concat_axis=0, tiled=True)
+    back = back.reshape(4, 4, 4, 32, ROWS).transpose(2, 0, 1, 3, 4).reshape(16, 128, ROWS)
+    back = lax.all_to_all(back, ("y", "x"), split_axis=0, concat_axis=0, tiled=True)
+    back = back.reshape(4, 4, 128, ROWS)
     return last_stage(back, right_whole), first_new, second_new
 
 

time: 211 us -> 213 us (level)
  waiting for transfers between devices: 64.2 us -> 67.8 us
  blocking collectives: 71.3 us -> 68.6 us
    all_to_all x1, blocking collectives: 34.9 us -> 30.8 us  [on_device(): lax.all_to_all(back.reshape(16, 128, ROWS), ZC, split_axis=0, concat_axis...]
    all_gather x2, waiting for transfers between devices: 2.42 us -> 5.33 us  [gather_whole(): whole = lax.all_gather(line.reshape(-1, BLOCK), XY, axis=0, tiled=True)]
where the time goes in v5:
time: 213 us; the launch traced here: 211 us
  blocking collectives  68.6 us (32%)
  waiting for transfers between devices  67.8 us (32%)
  starting transfers between devices  35.7 us (17%)
  Pallas kernels  17.5 us (8%)
  between operations  14.2 us (7%)
  local copies, waits for them, and re-layouts  3.84 us (2%)
  other arithmetic  3.55 us (2%)
    all_to_all x1, blocking collectives, on_device(): lax.all_to_all(moved, ('zh', 'y', 'zl'), split_axis=0, concat_axis=0, til...  37.8 us
    all_to_all x1, blocking collectives, on_device(): lax.all_to_all(back.reshape(16, 128, ROWS), ZC, split_axis=0, concat_axis...  30.8 us
    ppermute x15, waiting for transfers between devices, shift(): return lax.ppermute(value, axis, [(i, (i + by) % 4) for i in range(4)])  27.8 us
    ppermute x15, starting transfers between devices, shift(): return lax.ppermute(value, axis, [(i, (i + by) % 4) for i in range(4)])  22.8 us
    ppermute x2, waiting for transfers between devices, on_device(): moved.append(lax.ppermute(sent[t], ('x', 'core'), pairs))  18.8 us
    all_to_all x1, waiting for transfers between devices, on_device(): lax.all_to_all(back, ('y', 'x'), split_axis=0, concat_axis=0, tiled=True)  14.1 us
    pallas_call x1, Pallas kernels, middle_stage(): pl.pallas_call(middle_kernel, out_shape=(jax.ShapeDtypeStruct((16, 4, 32,...  10 us
    ppermute x2, starting transfers between devices, on_device(): moved.append(lax.ppermute(sent[t], ('x', 'core'), pairs))  5.86 us
  transfers between devices with their start and end apart: 21, of which 12 were waited for; matrix products, arithmetic and copies ran while one was open for 3% of the time, Pallas kernels for 6%

profile of v5, /device:TPU:1, one launch (start us, length us, event | category | flops | bytes accessed | tf_op | source)
XLA Modules:
  0.0 211.2 jit_solution(17325238160369747721)
XLA Ops:
  8.2 2.5 %collective-permute-start.1 = (bf16[6,16,1024]{2,1,0:T(8,128)(2,1)S(1)}, bf16[6,16,1024]{2,1,0:T(8,128)(2,1)S(1)}, u32[]{:S(2)}, u32[]{:S(2)}) collective-permute-start(bf16[6,16,1024]{2,1,0:T(8,128)(2,1)S(1)} %pad_select_fusion), channel_id=1, source_target_pairs={{0,4},{4,8},{8,12},{12,0},{1,5},{5,9},{9,13},{13,1},{2,6},{6,10},{... | collective-permute-start | bytes 589832 | tf_op jit(solution)/shard_map/ppermute | solution.py:23
  10.8 3.0 %collective-permute-start.2 = (bf16[6,16,1024]{2,1,0:T(8,128)(2,1)S(1)}, bf16[6,16,1024]{2,1,0:T(8,128)(2,1)S(1)}, u32[]{:S(2)}, u32[]{:S(2)}) collective-permute-start(bf16[6,16,1024]{2,1,0:T(8,128)(2,1)S(1)} %pad_select_fusion), channel_id=1, source_target_pairs={{0,8},{4,12},{8,0},{12,4},{1,9},{5,13},{9,1},{13,5},{2,10},{6,14},... | collective-permute-start | bytes 589832 | tf_op jit(solution)/shard_map/ppermute | solution.py:23
  14.5 1.3 broadcast_select_fusion
  15.8 2.8 %collective-permute-start = (bf16[256,1024]{1,0:T(8,128)(2,1)S(1)}, bf16[256,1024]{1,0:T(8,128)(2,1)S(1)}, u32[]{:S(2)}, u32[]{:S(2)}) collective-permute-start(bf16[256,1024]{1,0:T(8,128)(2,1)S(1)} %get-tuple-element.25), channel_id=1, source_target_pairs={{0,128},{64,192},{128,0},{192,64},{1,129},{65,193},{129,1},{193,65... | collective-permute-start | bytes 1572872 | tf_op jit(solution)/shard_map/ppermute | solution.py:192
  18.6 8.7 %collective-permute-done.2 = bf16[6,16,1024]{2,1,0:T(8,128)(2,1)S(1)} collective-permute-done((bf16[6,16,1024]{2,1,0:T(8,128)(2,1)S(1)}, bf16[6,16,1024]{2,1,0:T(8,128)(2,1)S(1)}, u32[]{:S(2)}, u32[]{:S(2)}) %collective-permute-start.2) | collective-permute-done | bytes 196640 | tf_op jit(solution)/shard_map/ppermute | solution.py:23
  27.6 1.7 collective-permute-done.given
  30.2 1.3 collective-permute-start.4
  31.5 1.5 collective-permute-start.5
  32.9 1.5 collective-permute-start.6
  34.5 1.4 collective-permute-start.7
  35.9 1.5 collective-permute-start.8
  37.4 1.6 collective-permute-start.9
  39.7 3.1 %collective-permute-done.9 = bf16[2,32,1024]{2,1,0:T(8,128)(2,1)S(1)} collective-permute-done((bf16[2,32,1024]{2,1,0:T(8,128)(2,1)S(1)}, bf16[2,32,1024]{2,1,0:T(8,128)(2,1)S(1)}, u32[]{:S(2)}, u32[]{:S(2)}) %collective-permute-start.9) | collective-permute-done | bytes 131104 | tf_op jit(solution)/shard_map/ppermute | solution.py:23
  44.0 2.4 %collective-permute-start.14 = (bf16[4,32,1024]{2,1,0:T(8,128)(2,1)}, bf16[4,32,1024]{2,1,0:T(8,128)(2,1)S(1)}, u32[]{:S(2)}, u32[]{:S(2)}) collective-permute-start(bf16[4,32,1024]{2,1,0:T(8,128)(2,1)} %get-tuple-element.38), channel_id=1, source_target_pairs={{0,192},{64,0},{128,64},{192,128},{1,193},{65,1},{129,65},{193,129... | collective-permute-start | bytes 786440 | tf_op jit(solution)/shard_map/ppermute | solution.py:23
  46.9 2.4 %collective-permute-start.11 = (bf16[4,32,1024]{2,1,0:T(8,128)(2,1)S(1)}, bf16[4,32,1024]{2,1,0:T(8,128)(2,1)S(1)}, u32[]{:S(2)}, u32[]{:S(2)}) collective-permute-start(bf16[4,32,1024]{2,1,0:T(8,128)(2,1)S(1)} %pad_maximum_fusion.3.refs_0_), channel_id=1, source_target_pairs={{0,48},{16,0},{32,16},{48,32},{1,49},{17,1},{33,17},{49,33},{2,50}... | collective-permute-start | bytes 786440 | tf_op jit(solution)/shard_map/ppermute | solution.py:23
  50.1 2.2 %collective-permute-start.12 = (bf16[4,32,1024]{2,1,0:T(8,128)(2,1)S(1)}, bf16[4,32,1024]{2,1,0:T(8,128)(2,1)S(1)}, u32[]{:S(2)}, u32[]{:S(2)}) collective-permute-start(bf16[4,32,1024]{2,1,0:T(8,128)(2,1)S(1)} %pad_maximum_fusion.3.refs_0_), channel_id=1, source_target_pairs={{0,32},{16,48},{32,0},{48,16},{1,33},{17,49},{33,1},{49,17},{2,34}... | collective-permute-start | bytes 786440 | tf_op jit(solution)/shard_map/ppermute | solution.py:23
  52.4 5.6 %collective-permute-done.14.refs_6_ = bf16[4,32,1024]{2,1,0:T(8,128)(2,1)S(1)} collective-permute-done((bf16[4,32,1024]{2,1,0:T(8,128)(2,1)}, bf16[4,32,1024]{2,1,0:T(8,128)(2,1)S(1)}, u32[]{:S(2)}, u32[]{:S(2)}) %collective-permute-start.14) | collective-permute-done | bytes 262176 | tf_op jit(solution)/shard_map/ppermute | solution.py:23
  58.0 2.9 %collective-permute-done.15.refs_7_ = bf16[4,32,1024]{2,1,0:T(8,128)(2,1)S(1)} collective-permute-done((bf16[4,32,1024]{2,1,0:T(8,128)(2,1)S(1)}, bf16[4,32,1024]{2,1,0:T(8,128)(2,1)S(1)}, u32[]{:S(2)}, u32[]{:S(2)}) %collective-permute-start.15) | collective-permute-done | bytes 262176 | tf_op jit(solution)/shard_map/ppermute | solution.py:23
  61.0 5.9 %collective-permute-done.12.refs_3_ = bf16[4,32,1024]{2,1,0:T(8,128)(2,1)S(1)} collective-permute-done((bf16[4,32,1024]{2,1,0:T(8,128)(2,1)S(1)}, bf16[4,32,1024]{2,1,0:T(8,128)(2,1)S(1)}, u32[]{:S(2)}, u32[]{:S(2)}) %collective-permute-start.12) | collective-permute-done | bytes 262176 | tf_op jit(solution)/shard_map/ppermute | solution.py:23
  66.9 2.4 %rotate_columns.1 = bf16[2,2,16,32,256]{4,3,2,1,0:T(8,128)(2,1)S(1)} custom-call(s32[4]{0:T(128)S(1)} %pad_add_fusion.place, bf16[256,1024]{1,0:T(8,128)(2,1)S(1)} %get-tuple-element.26.kept, bf16[256,1024]{1,0:T(8,128)(2,1)S(1)} %collective-permute-done.given, bf16[4,32,1024]{2,1,0:T(8,128)(2,1)S(1)} %pad_maximum_fusion.3.refs_0_, ...), custom_call_target="tpu_custom_call" | custom-call | flops 1073741824 | bytes 4194304 | tf_op jit(solution)/shard_map/rotate_columns/pallas_call | solution.py:68
  69.4 5.8 %collective-permute-start.16 = (bf16[2,16,32,256]{3,2,1,0:T(8,128)(2,1)S(1)}, bf16[2,16,32,256]{3,2,1,0:T(8,128)(2,1)S(1)}, u32[]{:S(2)}, u32[]{:S(2)}) collective-permute-start(bf16[2,16,32,256]{3,2,1,0:T(8,128)(2,1)S(1)} %get-tuple-element.24), channel_id=1, source_target_pairs={{0,0},{1,64},{64,1},{65,65},{128,128},{129,192},{192,129},{193,193... | collective-permute-start | bytes 1572872 | tf_op jit(solution)/shard_map/ppermute | solution.py:218
  75.3 1.7 slice.63
  77.0 16.0 %collective-permute-done.16 = bf16[2,16,32,256]{3,2,1,0:T(8,128)(2,1)S(1)} collective-permute-done((bf16[2,16,32,256]{3,2,1,0:T(8,128)(2,1)S(1)}, bf16[2,16,32,256]{3,2,1,0:T(8,128)(2,1)S(1)}, u32[]{:S(2)}, u32[]{:S(2)}) %collective-permute-start.16) | collective-permute-done | bytes 524320 | tf_op jit(solution)/shard_map/ppermute | solution.py:218
  93.1 2.8 %collective-permute-done.17 = bf16[2,16,32,256]{3,2,1,0:T(8,128)(2,1)S(1)} collective-permute-done((bf16[2,16,32,256]{3,2,1,0:T(8,128)(2,1)S(1)}, bf16[2,16,32,256]{3,2,1,0:T(8,128)(2,1)S(1)}, u32[]{:S(2)}, u32[]{:S(2)}) %collective-permute-start.17) | collective-permute-done | bytes 524320 | tf_op jit(solution)/shard_map/ppermute | solution.py:218
  96.1 37.8 %all_to_all.15 = bf16[32,64,256]{2,1,0:T(8,128)(2,1)S(1)} all-to-all(bf16[32,64,256]{2,1,0:T(8,128)(2,1)S(1)} %bitcast.68), channel_id=1, replica_groups=mesh['x'=4,'y'=4,'zl'=4,'zh'=2,'core'=2] {'zh','y','zl'}, dimensions={0} | all-to-all | bytes 2097152 | tf_op jit(solution)/shard_map/all_to_all | solution.py:221
  133.8 10.0 %moments_and_direction.1 = (bf16[16,4,32,256]{3,2,1,0:T(8,128)(2,1)S(1)}, f32[4096,128]{1,0:T(8,128)}, f32[4096,128]{1,0:T(8,128)}) custom-call(s32[4]{0:T(128)S(1)} %pad_add_fusion.place, bf16[2,4,8,32,256]{4,3,2,1,0:T(8,128)(2,1)S(1)} %bitcast.60, bf16[16,4,64,1024]{3,2,1,0:T(8,128)(2,1)} %bitcast.62, f32[4096,128]{1,0:T(8,128)} %first.1, f32[4096,128]{1,0:T(8,128)} %second.1), custom_call_target="tpu_custom_call" | custom-call | flops 2147483648 | bytes 18874368 | tf_op jit(solution)/shard_map/moments_and_direction/pallas_call | solution.py:120
  143.9 30.8 %all_to_all.16 = bf16[16,128,256]{2,1,0:T(8,128)(2,1)S(1)} all-to-all(bf16[16,128,256]{2,1,0:T(8,128)(2,1)S(1)} %bitcast.61), channel_id=1, replica_groups=mesh['x'=4,'y'=4,'zl'=4,'zh'=2,'core'=2] {'zh','core','zl'}, dimensions={0} | all-to-all | bytes 2097152 | tf_op jit(solution)/shard_map/all_to_all | solution.py:231
  174.7 1.1 copy.18
  175.8 4.1 %all-to-all-start.2 = ((bf16[16,128,256]{2,1,0:T(8,128)(2,1)}), bf16[16,128,256]{2,1,0:T(8,128)(2,1)S(1)}, u32[]{:S(2)}, u32[]{:S(2)}) async-start(bf16[16,128,256]{2,1,0:T(8,128)(2,1)} %bitcast.37), calls=%async_computation.2 | async-start | bytes 2097152 | tf_op jit(solution)/shard_map/all_to_all | solution.py:235
  179.9 5.3 %all-gather.5.cloned.1.call-done = bf16[2048,1024]{1,0:T(8,128)(2,1)} async-done(((bf16[128,1024]{1,0:T(8,128)(2,1)}), bf16[2048,1024]{1,0:T(8,128)(2,1)}) %all-gather.5.cloned.1.call-update) | async-done | bytes 4194320 | tf_op jit(solution)/shard_map/all_gather | solution.py:176
  185.2 14.1 %all-to-all-done.2 = bf16[16,128,256]{2,1,0:T(8,128)(2,1)S(1)} async-done(((bf16[16,128,256]{2,1,0:T(8,128)(2,1)}), bf16[16,128,256]{2,1,0:T(8,128)(2,1)S(1)}, u32[]{:S(2)}, u32[]{:S(2)}) %all-to-all-start.2) | async-done | bytes 1048608 | tf_op jit(solution)/shard_map/all_to_all | solution.py:235
  199.3 5.1 %rotate_back_columns.1 = f32[256,2048]{1,0:T(8,128)} custom-call(bf16[4,4,128,256]{3,2,1,0:T(8,128)(2,1)S(1)} %bitcast.59, bf16[16,2,64,1024]{3,2,1,0:T(8,128)(2,1)} %bitcast.67), custom_call_target="tpu_custom_call" | custom-call | flops 1073741824 | bytes 7340032 | tf_op jit(solution)/shard_map/rotate_back_columns/pallas_call | solution.py:158
  (37 shorter events, 6.7 us)
Async XLA Ops:
  7.2 126.7 %all-gather.3.cloned.1.call-start = ((), (), s32[]{:S(2)}) async-start(), calls=%async_computation.3 | async-start | bytes 8912896 | tf_op jit(solution)/shard_map/all_gather | solution.py:176
  8.2 10.4 %collective-permute-start.1 = (bf16[6,16,1024]{2,1,0:T(8,128)(2,1)S(1)}, bf16[6,16,1024]{2,1,0:T(8,128)(2,1)S(1)}, u32[]{:S(2)}, u32[]{:S(2)}) collective-permute-start(bf16[6,16,1024]{2,1,0:T(8,128)(2,1)S(1)} %pad_select_fusion), channel_id=1, source_target_pairs={{0,4},{4,8},{8,12},{12,0},{1,5},{5,9},{9,13},{13,1},{2,6},{6,10},{... | collective-permute-start | bytes 589832 | tf_op jit(solution)/shard_map/ppermute | solution.py:23
  10.8 16.5 %collective-permute-start.2 = (bf16[6,16,1024]{2,1,0:T(8,128)(2,1)S(1)}, bf16[6,16,1024]{2,1,0:T(8,128)(2,1)S(1)}, u32[]{:S(2)}, u32[]{:S(2)}) collective-permute-start(bf16[6,16,1024]{2,1,0:T(8,128)(2,1)S(1)} %pad_select_fusion), channel_id=1, source_target_pairs={{0,8},{4,12},{8,0},{12,4},{1,9},{5,13},{9,1},{13,5},{2,10},{6,14},... | collective-permute-start | bytes 589832 | tf_op jit(solution)/shard_map/ppermute | solution.py:23
  13.8 13.5 %collective-permute-start.3 = (bf16[6,16,1024]{2,1,0:T(8,128)(2,1)S(1)}, bf16[6,16,1024]{2,1,0:T(8,128)(2,1)S(1)}, u32[]{:S(2)}, u32[]{:S(2)}) collective-permute-start(bf16[6,16,1024]{2,1,0:T(8,128)(2,1)S(1)} %pad_select_fusion), channel_id=1, source_target_pairs={{0,12},{4,0},{8,4},{12,8},{1,13},{5,1},{9,5},{13,9},{2,14},{6,2},{... | collective-permute-start | bytes 589832 | tf_op jit(solution)/shard_map/ppermute | solution.py:23
  15.8 13.5 %collective-permute-start = (bf16[256,1024]{1,0:T(8,128)(2,1)S(1)}, bf16[256,1024]{1,0:T(8,128)(2,1)S(1)}, u32[]{:S(2)}, u32[]{:S(2)}) collective-permute-start(bf16[256,1024]{1,0:T(8,128)(2,1)S(1)} %get-tuple-element.25), channel_id=1, source_target_pairs={{0,128},{64,192},{128,0},{192,64},{1,129},{65,193},{129,1},{193,65... | collective-permute-start | bytes 1572872 | tf_op jit(solution)/shard_map/ppermute | solution.py:192
  27.5 16.1 %copy-start = (bf16[6,4,16,1024]{3,2,1,0:T(8,128)(2,1)}, bf16[6,4,16,1024]{3,2,1,0:T(8,128)(2,1)S(1)}, u32[]{:S(2)}) copy-start(bf16[6,4,16,1024]{3,2,1,0:T(8,128)(2,1)S(1)} %copy.13) | copy-start | bytes 2359300
  30.1 155.1 %all-gather.5.cloned.1.call-start = ((), (), s32[]{:S(2)}) async-start(), calls=%async_computation.4 | async-start | bytes 4456448 | tf_op jit(solution)/shard_map/all_gather | solution.py:176
  30.2 7.2 %collective-permute-start.4 = (bf16[32,1024]{1,0:T(8,128)(2,1)S(1)}, bf16[32,1024]{1,0:T(8,128)(2,1)S(1)}, u32[]{:S(2)}, u32[]{:S(2)}) collective-permute-start(bf16[32,1024]{1,0:T(8,128)(2,1)S(1)} %get-tuple-element.32), channel_id=1, source_target_pairs={{0,64},{64,128},{128,192},{192,0},{1,65},{65,129},{129,193},{193,1... | collective-permute-start | bytes 196616 | tf_op jit(solution)/shard_map/ppermute | solution.py:23
  31.5 7.5 %collective-permute-start.5 = (bf16[32,1024]{1,0:T(8,128)(2,1)S(1)}, bf16[32,1024]{1,0:T(8,128)(2,1)S(1)}, u32[]{:S(2)}, u32[]{:S(2)}) collective-permute-start(bf16[32,1024]{1,0:T(8,128)(2,1)S(1)} %get-tuple-element.30), channel_id=1, source_target_pairs={{0,192},{64,0},{128,64},{192,128},{1,193},{65,1},{129,65},{193,129... | collective-permute-start | bytes 196616 | tf_op jit(solution)/shard_map/ppermute | solution.py:23
  32.9 6.0 %collective-permute-start.6 = (bf16[32,1024]{1,0:T(8,128)(2,1)S(1)}, bf16[32,1024]{1,0:T(8,128)(2,1)S(1)}, u32[]{:S(2)}, u32[]{:S(2)}) collective-permute-start(bf16[32,1024]{1,0:T(8,128)(2,1)S(1)} %get-tuple-element.31), channel_id=1, source_target_pairs={{0,128},{64,192},{128,0},{192,64},{1,129},{65,193},{129,1},{193,65... | collective-permute-start | bytes 196616 | tf_op jit(solution)/shard_map/ppermute | solution.py:23
  34.5 5.2 %collective-permute-start.7 = (bf16[2,32,1024]{2,1,0:T(8,128)(2,1)S(1)}, bf16[2,32,1024]{2,1,0:T(8,128)(2,1)S(1)}, u32[]{:S(2)}, u32[]{:S(2)}) collective-permute-start(bf16[2,32,1024]{2,1,0:T(8,128)(2,1)S(1)} %get-tuple-element.28), channel_id=1, source_target_pairs={{0,16},{16,32},{32,48},{48,0},{1,17},{17,33},{33,49},{49,1},{2,18}... | collective-permute-start | bytes 393224 | tf_op jit(solution)/shard_map/ppermute | solution.py:23
  35.9 3.8 %collective-permute-start.8 = (bf16[2,32,1024]{2,1,0:T(8,128)(2,1)S(1)}, bf16[2,32,1024]{2,1,0:T(8,128)(2,1)S(1)}, u32[]{:S(2)}, u32[]{:S(2)}) collective-permute-start(bf16[2,32,1024]{2,1,0:T(8,128)(2,1)S(1)} %get-tuple-element.28), channel_id=1, source_target_pairs={{0,48},{16,0},{32,16},{48,32},{1,49},{17,1},{33,17},{49,33},{2,50}... | collective-permute-start | bytes 393224 | tf_op jit(solution)/shard_map/ppermute | solution.py:23
  37.4 5.4 %collective-permute-start.9 = (bf16[2,32,1024]{2,1,0:T(8,128)(2,1)S(1)}, bf16[2,32,1024]{2,1,0:T(8,128)(2,1)S(1)}, u32[]{:S(2)}, u32[]{:S(2)}) collective-permute-start(bf16[2,32,1024]{2,1,0:T(8,128)(2,1)S(1)} %get-tuple-element.28), channel_id=1, source_target_pairs={{0,32},{16,48},{32,0},{48,16},{1,33},{17,49},{33,1},{49,17},{2,34}... | collective-permute-start | bytes 393224 | tf_op jit(solution)/shard_map/ppermute | solution.py:23
  43.7 6.5 %collective-permute-start.13 = (bf16[4,32,1024]{2,1,0:T(8,128)(2,1)S(1)}, bf16[4,32,1024]{2,1,0:T(8,128)(2,1)S(1)}, u32[]{:S(2)}, u32[]{:S(2)}) collective-permute-start(bf16[4,32,1024]{2,1,0:T(8,128)(2,1)S(1)} %get-tuple-element.40), channel_id=1, source_target_pairs={{0,64},{64,128},{128,192},{192,0},{1,65},{65,129},{129,193},{193,1... | collective-permute-start | bytes 786440 | tf_op jit(solution)/shard_map/ppermute | solution.py:23
  44.0 14.1 %collective-permute-start.14 = (bf16[4,32,1024]{2,1,0:T(8,128)(2,1)}, bf16[4,32,1024]{2,1,0:T(8,128)(2,1)S(1)}, u32[]{:S(2)}, u32[]{:S(2)}) collective-permute-start(bf16[4,32,1024]{2,1,0:T(8,128)(2,1)} %get-tuple-element.38), channel_id=1, source_target_pairs={{0,192},{64,0},{128,64},{192,128},{1,193},{65,1},{129,65},{193,129... | collective-permute-start | bytes 786440 | tf_op jit(solution)/shard_map/ppermute | solution.py:23
  46.3 14.6 %collective-permute-start.15 = (bf16[4,32,1024]{2,1,0:T(8,128)(2,1)S(1)}, bf16[4,32,1024]{2,1,0:T(8,128)(2,1)S(1)}, u32[]{:S(2)}, u32[]{:S(2)}) collective-permute-start(bf16[4,32,1024]{2,1,0:T(8,128)(2,1)S(1)} %get-tuple-element.37), channel_id=1, source_target_pairs={{0,128},{64,192},{128,0},{192,64},{1,129},{65,193},{129,1},{193,65... | collective-permute-start | bytes 786440 | tf_op jit(solution)/shard_map/ppermute | solution.py:23
  46.6 14.4 %collective-permute-start.10 = (bf16[4,32,1024]{2,1,0:T(8,128)(2,1)S(1)}, bf16[4,32,1024]{2,1,0:T(8,128)(2,1)S(1)}, u32[]{:S(2)}, u32[]{:S(2)}) collective-permute-start(bf16[4,32,1024]{2,1,0:T(8,128)(2,1)S(1)} %pad_maximum_fusion.3.refs_0_), channel_id=1, source_target_pairs={{0,16},{16,32},{32,48},{48,0},{1,17},{17,33},{33,49},{49,1},{2,18}... | collective-permute-start | bytes 786440 | tf_op jit(solution)/shard_map/ppermute | solution.py:23
  46.9 14.1 %collective-permute-start.11 = (bf16[4,32,1024]{2,1,0:T(8,128)(2,1)S(1)}, bf16[4,32,1024]{2,1,0:T(8,128)(2,1)S(1)}, u32[]{:S(2)}, u32[]{:S(2)}) collective-permute-start(bf16[4,32,1024]{2,1,0:T(8,128)(2,1)S(1)} %pad_maximum_fusion.3.refs_0_), channel_id=1, source_target_pairs={{0,48},{16,0},{32,16},{48,32},{1,49},{17,1},{33,17},{49,33},{2,50}... | collective-permute-start | bytes 786440 | tf_op jit(solution)/shard_map/ppermute | solution.py:23
  50.1 16.8 %collective-permute-start.12 = (bf16[4,32,1024]{2,1,0:T(8,128)(2,1)S(1)}, bf16[4,32,1024]{2,1,0:T(8,128)(2,1)S(1)}, u32[]{:S(2)}, u32[]{:S(2)}) collective-permute-start(bf16[4,32,1024]{2,1,0:T(8,128)(2,1)S(1)} %pad_maximum_fusion.3.refs_0_), channel_id=1, source_target_pairs={{0,32},{16,48},{32,0},{48,16},{1,33},{17,49},{33,1},{49,17},{2,34}... | collective-permute-start | bytes 786440 | tf_op jit(solution)/shard_map/ppermute | solution.py:23
  69.4 23.6 %collective-permute-start.16 = (bf16[2,16,32,256]{3,2,1,0:T(8,128)(2,1)S(1)}, bf16[2,16,32,256]{3,2,1,0:T(8,128)(2,1)S(1)}, u32[]{:S(2)}, u32[]{:S(2)}) collective-permute-start(bf16[2,16,32,256]{3,2,1,0:T(8,128)(2,1)S(1)} %get-tuple-element.24), channel_id=1, source_target_pairs={{0,0},{1,64},{64,1},{65,65},{128,128},{129,192},{192,129},{193,193... | collective-permute-start | bytes 1572872 | tf_op jit(solution)/shard_map/ppermute | solution.py:218
  75.2 20.6 %collective-permute-start.17 = (bf16[2,16,32,256]{3,2,1,0:T(8,128)(2,1)S(1)}, bf16[2,16,32,256]{3,2,1,0:T(8,128)(2,1)S(1)}, u32[]{:S(2)}, u32[]{:S(2)}) collective-permute-start(bf16[2,16,32,256]{3,2,1,0:T(8,128)(2,1)S(1)} %get-tuple-element.23), channel_id=1, source_target_pairs={{0,64},{1,0},{64,65},{65,1},{128,192},{129,128},{192,193},{193,129... | collective-permute-start | bytes 1572872 | tf_op jit(solution)/shard_map/ppermute | solution.py:218
  175.8 23.5 %all-to-all-start.2 = ((bf16[16,128,256]{2,1,0:T(8,128)(2,1)}), bf16[16,128,256]{2,1,0:T(8,128)(2,1)S(1)}, u32[]{:S(2)}, u32[]{:S(2)}) async-start(bf16[16,128,256]{2,1,0:T(8,128)(2,1)} %bitcast.37), calls=%async_computation.2 | async-start | bytes 2097152 | tf_op jit(solution)/shard_map/all_to_all | solution.py:235
Sparse Core Ops, SparseCore 0:
  30.2 93.3 all-gather.2
  126.1 59.1 all-gather.4

commit v6 on v4

--- a/solution.py
+++ b/solution.py
@@ -87,7 +87,7 @@
 
 
 def middle_kernel(place, owned, left_block, first, second, back, first_out, second_out):
-    left = left_block[:, 0].reshape(BLOCK, BLOCK)
+    left = jnp.concatenate([left_block[y, x, 0] for x in range(4) for y in range(4)], axis=0)
     low = place[0] & 1
     columns = jnp.concatenate(
         [
@@ -128,7 +128,7 @@
             grid=(4,),
             in_specs=[
                 pl.BlockSpec((1, 16, 32, ROWS), lambda b, place: (b, 0, 0, 0)),
-                pl.BlockSpec((16, 1, 64, BLOCK), lambda b, place: (0, b, 0, 0)),
+                pl.BlockSpec((4, 4, 1, 64, BLOCK), lambda b, place: (0, 0, b, 0, 0)),
                 moments,
                 moments,
             ],
@@ -147,7 +147,7 @@
 def last_kernel(back, right_whole, update):
     update[...] = lax.dot_general(
         back[...].reshape(BLOCK, ROWS).T,
-        right_whole[:, 0].reshape(BLOCK // 2, BLOCK),
+        jnp.concatenate([right_whole[y, x, 0] for x in range(2) for y in range(4)], axis=0),
         (((1,), (1,)), ((), ())),
         preferred_element_type=jnp.float32,
     )
@@ -160,7 +160,7 @@
         grid=(2, 2),
         in_specs=[
             pl.BlockSpec((8, 128, ROWS), lambda k, i: (k, 0, 0)),
-            pl.BlockSpec((8, 1, 64, BLOCK), lambda k, i: (i, k, 0, 0)),
+            pl.BlockSpec((4, 2, 1, 64, BLOCK), lambda k, i: (0, i, k, 0, 0)),
         ],
         out_specs=pl.BlockSpec((ROWS, BLOCK // 2), lambda k, i: (0, 2 * k + i)),
         compiler_params=pltpu.CompilerParams(vmem_limit_bytes=VMEM_LIMIT),
@@ -172,8 +172,8 @@
 
 
 def gather_whole(line):
-    whole = lax.all_gather(line.reshape(-1, BLOCK), XY, axis=0, tiled=True)
-    return whole.reshape(16, *line.shape)
+    whole = lax.all_gather(line.reshape(-1, BLOCK), ("y", "x"), axis=0, tiled=True)
+    return whole.reshape(4, 4, *line.shape)
 
 
 def on_device(grad, right_basis, left_basis, first_moment, second_moment):

time: 211 us -> 211 us (level)
  no operation moved by 1% of the time
where the time goes in v6:
time: 211 us; the launch traced here: 210 us
  blocking collectives  71.3 us (34%)
  waiting for transfers between devices  64.2 us (30%)
  starting transfers between devices  35.9 us (17%)
  Pallas kernels  17.3 us (8%)
  between operations  14.2 us (7%)
  local copies, waits for them, and re-layouts  3.83 us (2%)
  other arithmetic  3.55 us (2%)
    all_to_all x1, blocking collectives, on_device(): lax.all_to_all(moved, ('y', 'zl', 'zh'), split_axis=0, concat_axis=0, til...  36.4 us
    all_to_all x1, blocking collectives, on_device(): lax.all_to_all(back.reshape(16, 128, ROWS), ZC, split_axis=0, concat_axis...  34.9 us
    ppermute x15, waiting for transfers between devices, shift(): return lax.ppermute(value, axis, [(i, (i + by) % 4) for i in range(4)])  27.8 us
    ppermute x15, starting transfers between devices, shift(): return lax.ppermute(value, axis, [(i, (i + by) % 4) for i in range(4)])  22.8 us
    ppermute x2, waiting for transfers between devices, on_device(): moved.append(lax.ppermute(sent[t], ('x', 'core'), pairs))  18.8 us
    all_to_all x1, waiting for transfers between devices, on_device(): back = lax.all_to_all(back, XY, split_axis=0, concat_axis=0, tiled=True)  13.4 us
    pallas_call x1, Pallas kernels, middle_stage(): pl.pallas_call(middle_kernel, out_shape=(jax.ShapeDtypeStruct((16, 4, 32,...  9.88 us
    ppermute x2, starting transfers between devices, on_device(): moved.append(lax.ppermute(sent[t], ('x', 'core'), pairs))  5.86 us
  transfers between devices with their start and end apart: 21, of which 12 were waited for; matrix products, arithmetic and copies ran while one was open for 3% of the time, Pallas kernels for 6%

profile of v6, /device:TPU:1, one launch (start us, length us, event | category | flops | bytes accessed | tf_op | source)
XLA Modules:
  0.0 210.3 jit_solution(17991023516443980995)
XLA Ops:
  8.2 2.5 %collective-permute-start.1 = (bf16[6,16,1024]{2,1,0:T(8,128)(2,1)S(1)}, bf16[6,16,1024]{2,1,0:T(8,128)(2,1)S(1)}, u32[]{:S(2)}, u32[]{:S(2)}) collective-permute-start(bf16[6,16,1024]{2,1,0:T(8,128)(2,1)S(1)} %pad_select_fusion), channel_id=1, source_target_pairs={{0,4},{4,8},{8,12},{12,0},{1,5},{5,9},{9,13},{13,1},{2,6},{6,10},{... | collective-permute-start | bytes 589832 | tf_op jit(solution)/shard_map/ppermute | solution.py:23
  10.8 3.0 %collective-permute-start.2 = (bf16[6,16,1024]{2,1,0:T(8,128)(2,1)S(1)}, bf16[6,16,1024]{2,1,0:T(8,128)(2,1)S(1)}, u32[]{:S(2)}, u32[]{:S(2)}) collective-permute-start(bf16[6,16,1024]{2,1,0:T(8,128)(2,1)S(1)} %pad_select_fusion), channel_id=1, source_target_pairs={{0,8},{4,12},{8,0},{12,4},{1,9},{5,13},{9,1},{13,5},{2,10},{6,14},... | collective-permute-start | bytes 589832 | tf_op jit(solution)/shard_map/ppermute | solution.py:23
  14.5 1.3 broadcast_select_fusion
  15.8 2.8 %collective-permute-start = (bf16[256,1024]{1,0:T(8,128)(2,1)S(1)}, bf16[256,1024]{1,0:T(8,128)(2,1)S(1)}, u32[]{:S(2)}, u32[]{:S(2)}) collective-permute-start(bf16[256,1024]{1,0:T(8,128)(2,1)S(1)} %get-tuple-element.25), channel_id=1, source_target_pairs={{0,128},{64,192},{128,0},{192,64},{1,129},{65,193},{129,1},{193,65... | collective-permute-start | bytes 1572872 | tf_op jit(solution)/shard_map/ppermute | solution.py:191
  18.6 8.7 %collective-permute-done.2 = bf16[6,16,1024]{2,1,0:T(8,128)(2,1)S(1)} collective-permute-done((bf16[6,16,1024]{2,1,0:T(8,128)(2,1)S(1)}, bf16[6,16,1024]{2,1,0:T(8,128)(2,1)S(1)}, u32[]{:S(2)}, u32[]{:S(2)}) %collective-permute-start.2) | collective-permute-done | bytes 196640 | tf_op jit(solution)/shard_map/ppermute | solution.py:23
  27.6 1.7 collective-permute-done.given
  30.2 1.3 collective-permute-start.4
  31.5 1.5 collective-permute-start.5
  32.9 1.5 collective-permute-start.6
  34.5 1.4 collective-permute-start.7
  35.9 1.5 collective-permute-start.8
  37.4 1.6 collective-permute-start.9
  39.7 3.1 %collective-permute-done.9 = bf16[2,32,1024]{2,1,0:T(8,128)(2,1)S(1)} collective-permute-done((bf16[2,32,1024]{2,1,0:T(8,128)(2,1)S(1)}, bf16[2,32,1024]{2,1,0:T(8,128)(2,1)S(1)}, u32[]{:S(2)}, u32[]{:S(2)}) %collective-permute-start.9) | collective-permute-done | bytes 131104 | tf_op jit(solution)/shard_map/ppermute | solution.py:23
  44.0 2.4 %collective-permute-start.14 = (bf16[4,32,1024]{2,1,0:T(8,128)(2,1)}, bf16[4,32,1024]{2,1,0:T(8,128)(2,1)S(1)}, u32[]{:S(2)}, u32[]{:S(2)}) collective-permute-start(bf16[4,32,1024]{2,1,0:T(8,128)(2,1)} %get-tuple-element.38), channel_id=1, source_target_pairs={{0,192},{64,0},{128,64},{192,128},{1,193},{65,1},{129,65},{193,129... | collective-permute-start | bytes 786440 | tf_op jit(solution)/shard_map/ppermute | solution.py:23
  46.9 2.4 %collective-permute-start.11 = (bf16[4,32,1024]{2,1,0:T(8,128)(2,1)S(1)}, bf16[4,32,1024]{2,1,0:T(8,128)(2,1)S(1)}, u32[]{:S(2)}, u32[]{:S(2)}) collective-permute-start(bf16[4,32,1024]{2,1,0:T(8,128)(2,1)S(1)} %pad_maximum_fusion.3.refs_0_), channel_id=1, source_target_pairs={{0,48},{16,0},{32,16},{48,32},{1,49},{17,1},{33,17},{49,33},{2,50}... | collective-permute-start | bytes 786440 | tf_op jit(solution)/shard_map/ppermute | solution.py:23
  50.1 2.2 %collective-permute-start.12 = (bf16[4,32,1024]{2,1,0:T(8,128)(2,1)S(1)}, bf16[4,32,1024]{2,1,0:T(8,128)(2,1)S(1)}, u32[]{:S(2)}, u32[]{:S(2)}) collective-permute-start(bf16[4,32,1024]{2,1,0:T(8,128)(2,1)S(1)} %pad_maximum_fusion.3.refs_0_), channel_id=1, source_target_pairs={{0,32},{16,48},{32,0},{48,16},{1,33},{17,49},{33,1},{49,17},{2,34}... | collective-permute-start | bytes 786440 | tf_op jit(solution)/shard_map/ppermute | solution.py:23
  52.4 5.6 %collective-permute-done.14.refs_6_ = bf16[4,32,1024]{2,1,0:T(8,128)(2,1)S(1)} collective-permute-done((bf16[4,32,1024]{2,1,0:T(8,128)(2,1)}, bf16[4,32,1024]{2,1,0:T(8,128)(2,1)S(1)}, u32[]{:S(2)}, u32[]{:S(2)}) %collective-permute-start.14) | collective-permute-done | bytes 262176 | tf_op jit(solution)/shard_map/ppermute | solution.py:23
  58.0 2.9 %collective-permute-done.15.refs_7_ = bf16[4,32,1024]{2,1,0:T(8,128)(2,1)S(1)} collective-permute-done((bf16[4,32,1024]{2,1,0:T(8,128)(2,1)S(1)}, bf16[4,32,1024]{2,1,0:T(8,128)(2,1)S(1)}, u32[]{:S(2)}, u32[]{:S(2)}) %collective-permute-start.15) | collective-permute-done | bytes 262176 | tf_op jit(solution)/shard_map/ppermute | solution.py:23
  61.0 5.9 %collective-permute-done.12.refs_3_ = bf16[4,32,1024]{2,1,0:T(8,128)(2,1)S(1)} collective-permute-done((bf16[4,32,1024]{2,1,0:T(8,128)(2,1)S(1)}, bf16[4,32,1024]{2,1,0:T(8,128)(2,1)S(1)}, u32[]{:S(2)}, u32[]{:S(2)}) %collective-permute-start.12) | collective-permute-done | bytes 262176 | tf_op jit(solution)/shard_map/ppermute | solution.py:23
  66.9 2.4 %rotate_columns.1 = bf16[2,16,2,32,256]{4,3,2,1,0:T(8,128)(2,1)S(1)} custom-call(s32[4]{0:T(128)S(1)} %pad_add_fusion.place, bf16[256,1024]{1,0:T(8,128)(2,1)S(1)} %get-tuple-element.26.kept, bf16[256,1024]{1,0:T(8,128)(2,1)S(1)} %collective-permute-done.given, bf16[4,32,1024]{2,1,0:T(8,128)(2,1)S(1)} %pad_maximum_fusion.3.refs_0_, ...), custom_call_target="tpu_custom_call" | custom-call | flops 1073741824 | bytes 4194304 | tf_op jit(solution)/shard_map/rotate_columns/pallas_call | solution.py:68
  69.4 5.8 %collective-permute-start.16 = (bf16[16,2,32,256]{3,2,1,0:T(8,128)(2,1)S(1)}, bf16[16,2,32,256]{3,2,1,0:T(8,128)(2,1)S(1)}, u32[]{:S(2)}, u32[]{:S(2)}) collective-permute-start(bf16[16,2,32,256]{3,2,1,0:T(8,128)(2,1)S(1)} %get-tuple-element.24), channel_id=1, source_target_pairs={{0,0},{1,64},{64,1},{65,65},{128,128},{129,192},{192,129},{193,193... | collective-permute-start | bytes 1572872 | tf_op jit(solution)/shard_map/ppermute | solution.py:217
  75.3 1.7 slice.63
  77.0 16.0 %collective-permute-done.16 = bf16[16,2,32,256]{3,2,1,0:T(8,128)(2,1)S(1)} collective-permute-done((bf16[16,2,32,256]{3,2,1,0:T(8,128)(2,1)S(1)}, bf16[16,2,32,256]{3,2,1,0:T(8,128)(2,1)S(1)}, u32[]{:S(2)}, u32[]{:S(2)}) %collective-permute-start.16) | collective-permute-done | bytes 524320 | tf_op jit(solution)/shard_map/ppermute | solution.py:217
  93.0 2.8 %collective-permute-done.17 = bf16[16,2,32,256]{3,2,1,0:T(8,128)(2,1)S(1)} collective-permute-done((bf16[16,2,32,256]{3,2,1,0:T(8,128)(2,1)S(1)}, bf16[16,2,32,256]{3,2,1,0:T(8,128)(2,1)S(1)}, u32[]{:S(2)}, u32[]{:S(2)}) %collective-permute-start.17) | collective-permute-done | bytes 524320 | tf_op jit(solution)/shard_map/ppermute | solution.py:217
  96.0 36.4 %all_to_all.15 = bf16[32,64,256]{2,1,0:T(8,128)(2,1)S(1)} all-to-all(bf16[32,64,256]{2,1,0:T(8,128)(2,1)S(1)} %bitcast.66), channel_id=1, replica_groups=mesh['x'=4,'y'=4,'zl'=4,'zh'=2,'core'=2] {'y','zl','zh'}, dimensions={0} | all-to-all | bytes 2097152 | tf_op jit(solution)/shard_map/all_to_all | solution.py:220
  132.4 9.9 %moments_and_direction.1 = (bf16[16,4,32,256]{3,2,1,0:T(8,128)(2,1)S(1)}, f32[4096,128]{1,0:T(8,128)}, f32[4096,128]{1,0:T(8,128)}) custom-call(s32[4]{0:T(128)S(1)} %pad_add_fusion.place, bf16[4,16,32,256]{3,2,1,0:T(8,128)(2,1)S(1)} %bitcast.58, bf16[4,4,4,64,1024]{4,3,2,1,0:T(8,128)(2,1)} %bitcast.60, f32[4096,128]{1,0:T(8,128)} %first.1, f32[4096,128]{1,0:T(8,128)} %second.1), custom_call_target="tpu_custom_call" | custom-call | flops 2147483648 | bytes 18874368 | tf_op jit(solution)/shard_map/moments_and_direction/pallas_call | solution.py:119
  142.3 34.9 %all_to_all.16 = bf16[16,128,256]{2,1,0:T(8,128)(2,1)S(1)} all-to-all(bf16[16,128,256]{2,1,0:T(8,128)(2,1)S(1)} %bitcast.59), channel_id=1, replica_groups=mesh['x'=4,'y'=4,'zl'=4,'zh'=2,'core'=2] {'zl','zh','core'}, dimensions={0} | all-to-all | bytes 2097152 | tf_op jit(solution)/shard_map/all_to_all | solution.py:230
  177.2 1.1 copy.17
  178.3 4.3 %all-to-all-start.2 = ((bf16[16,128,256]{2,1,0:T(8,128)(2,1)}), bf16[16,128,256]{2,1,0:T(8,128)(2,1)S(1)}, u32[]{:S(2)}, u32[]{:S(2)}) async-start(bf16[16,128,256]{2,1,0:T(8,128)(2,1)} %bitcast.37), calls=%async_computation.2 | async-start | bytes 2097152 | tf_op jit(solution)/shard_map/all_to_all | solution.py:234
  182.6 2.4 %all-gather.5.cloned.1.call-done = bf16[2048,1024]{1,0:T(8,128)(2,1)} async-done(((bf16[128,1024]{1,0:T(8,128)(2,1)}), bf16[2048,1024]{1,0:T(8,128)(2,1)}) %all-gather.5.cloned.1.call-update) | async-done | bytes 4194320 | tf_op jit(solution)/shard_map/all_gather | solution.py:175
  185.0 13.4 %all-to-all-done.2.back = bf16[16,128,256]{2,1,0:T(8,128)(2,1)S(1)} async-done(((bf16[16,128,256]{2,1,0:T(8,128)(2,1)}), bf16[16,128,256]{2,1,0:T(8,128)(2,1)S(1)}, u32[]{:S(2)}, u32[]{:S(2)}) %all-to-all-start.2) | async-done | bytes 1048608 | tf_op jit(solution)/shard_map/all_to_all | solution.py:234
  198.4 5.1 %rotate_back_columns.1 = f32[256,2048]{1,0:T(8,128)} custom-call(bf16[16,128,256]{2,1,0:T(8,128)(2,1)S(1)} %all-to-all-done.2.back, bf16[4,4,2,64,1024]{4,3,2,1,0:T(8,128)(2,1)} %bitcast.65), custom_call_target="tpu_custom_call" | custom-call | flops 1073741824 | bytes 7340032 | tf_op jit(solution)/shard_map/rotate_back_columns/pallas_call | solution.py:157
  (37 shorter events, 6.7 us)
Async XLA Ops:
  7.2 125.2 %all-gather.3.cloned.1.call-start = ((), (), s32[]{:S(2)}) async-start(), calls=%async_computation.3 | async-start | bytes 8912896 | tf_op jit(solution)/shard_map/all_gather | solution.py:175
  8.2 10.4 %collective-permute-start.1 = (bf16[6,16,1024]{2,1,0:T(8,128)(2,1)S(1)}, bf16[6,16,1024]{2,1,0:T(8,128)(2,1)S(1)}, u32[]{:S(2)}, u32[]{:S(2)}) collective-permute-start(bf16[6,16,1024]{2,1,0:T(8,128)(2,1)S(1)} %pad_select_fusion), channel_id=1, source_target_pairs={{0,4},{4,8},{8,12},{12,0},{1,5},{5,9},{9,13},{13,1},{2,6},{6,10},{... | collective-permute-start | bytes 589832 | tf_op jit(solution)/shard_map/ppermute | solution.py:23
  10.8 16.5 %collective-permute-start.2 = (bf16[6,16,1024]{2,1,0:T(8,128)(2,1)S(1)}, bf16[6,16,1024]{2,1,0:T(8,128)(2,1)S(1)}, u32[]{:S(2)}, u32[]{:S(2)}) collective-permute-start(bf16[6,16,1024]{2,1,0:T(8,128)(2,1)S(1)} %pad_select_fusion), channel_id=1, source_target_pairs={{0,8},{4,12},{8,0},{12,4},{1,9},{5,13},{9,1},{13,5},{2,10},{6,14},... | collective-permute-start | bytes 589832 | tf_op jit(solution)/shard_map/ppermute | solution.py:23
  13.8 13.5 %collective-permute-start.3 = (bf16[6,16,1024]{2,1,0:T(8,128)(2,1)S(1)}, bf16[6,16,1024]{2,1,0:T(8,128)(2,1)S(1)}, u32[]{:S(2)}, u32[]{:S(2)}) collective-permute-start(bf16[6,16,1024]{2,1,0:T(8,128)(2,1)S(1)} %pad_select_fusion), channel_id=1, source_target_pairs={{0,12},{4,0},{8,4},{12,8},{1,13},{5,1},{9,5},{13,9},{2,14},{6,2},{... | collective-permute-start | bytes 589832 | tf_op jit(solution)/shard_map/ppermute | solution.py:23
  15.8 13.5 %collective-permute-start = (bf16[256,1024]{1,0:T(8,128)(2,1)S(1)}, bf16[256,1024]{1,0:T(8,128)(2,1)S(1)}, u32[]{:S(2)}, u32[]{:S(2)}) collective-permute-start(bf16[256,1024]{1,0:T(8,128)(2,1)S(1)} %get-tuple-element.25), channel_id=1, source_target_pairs={{0,128},{64,192},{128,0},{192,64},{1,129},{65,193},{129,1},{193,65... | collective-permute-start | bytes 1572872 | tf_op jit(solution)/shard_map/ppermute | solution.py:191
  27.5 16.1 %copy-start = (bf16[6,4,16,1024]{3,2,1,0:T(8,128)(2,1)}, bf16[6,4,16,1024]{3,2,1,0:T(8,128)(2,1)S(1)}, u32[]{:S(2)}) copy-start(bf16[6,4,16,1024]{3,2,1,0:T(8,128)(2,1)S(1)} %copy.12) | copy-start | bytes 2359300
  30.1 154.9 %all-gather.5.cloned.1.call-start = ((), (), s32[]{:S(2)}) async-start(), calls=%async_computation.4 | async-start | bytes 4456448 | tf_op jit(solution)/shard_map/all_gather | solution.py:175
  30.2 7.2 %collective-permute-start.4 = (bf16[32,1024]{1,0:T(8,128)(2,1)S(1)}, bf16[32,1024]{1,0:T(8,128)(2,1)S(1)}, u32[]{:S(2)}, u32[]{:S(2)}) collective-permute-start(bf16[32,1024]{1,0:T(8,128)(2,1)S(1)} %get-tuple-element.32), channel_id=1, source_target_pairs={{0,64},{64,128},{128,192},{192,0},{1,65},{65,129},{129,193},{193,1... | collective-permute-start | bytes 196616 | tf_op jit(solution)/shard_map/ppermute | solution.py:23
  31.5 7.5 %collective-permute-start.5 = (bf16[32,1024]{1,0:T(8,128)(2,1)S(1)}, bf16[32,1024]{1,0:T(8,128)(2,1)S(1)}, u32[]{:S(2)}, u32[]{:S(2)}) collective-permute-start(bf16[32,1024]{1,0:T(8,128)(2,1)S(1)} %get-tuple-element.30), channel_id=1, source_target_pairs={{0,192},{64,0},{128,64},{192,128},{1,193},{65,1},{129,65},{193,129... | collective-permute-start | bytes 196616 | tf_op jit(solution)/shard_map/ppermute | solution.py:23
  32.9 6.0 %collective-permute-start.6 = (bf16[32,1024]{1,0:T(8,128)(2,1)S(1)}, bf16[32,1024]{1,0:T(8,128)(2,1)S(1)}, u32[]{:S(2)}, u32[]{:S(2)}) collective-permute-start(bf16[32,1024]{1,0:T(8,128)(2,1)S(1)} %get-tuple-element.31), channel_id=1, source_target_pairs={{0,128},{64,192},{128,0},{192,64},{1,129},{65,193},{129,1},{193,65... | collective-permute-start | bytes 196616 | tf_op jit(solution)/shard_map/ppermute | solution.py:23
  34.5 5.2 %collective-permute-start.7 = (bf16[2,32,1024]{2,1,0:T(8,128)(2,1)S(1)}, bf16[2,32,1024]{2,1,0:T(8,128)(2,1)S(1)}, u32[]{:S(2)}, u32[]{:S(2)}) collective-permute-start(bf16[2,32,1024]{2,1,0:T(8,128)(2,1)S(1)} %get-tuple-element.28), channel_id=1, source_target_pairs={{0,16},{16,32},{32,48},{48,0},{1,17},{17,33},{33,49},{49,1},{2,18}... | collective-permute-start | bytes 393224 | tf_op jit(solution)/shard_map/ppermute | solution.py:23
  35.9 3.8 %collective-permute-start.8 = (bf16[2,32,1024]{2,1,0:T(8,128)(2,1)S(1)}, bf16[2,32,1024]{2,1,0:T(8,128)(2,1)S(1)}, u32[]{:S(2)}, u32[]{:S(2)}) collective-permute-start(bf16[2,32,1024]{2,1,0:T(8,128)(2,1)S(1)} %get-tuple-element.28), channel_id=1, source_target_pairs={{0,48},{16,0},{32,16},{48,32},{1,49},{17,1},{33,17},{49,33},{2,50}... | collective-permute-start | bytes 393224 | tf_op jit(solution)/shard_map/ppermute | solution.py:23
  37.4 5.4 %collective-permute-start.9 = (bf16[2,32,1024]{2,1,0:T(8,128)(2,1)S(1)}, bf16[2,32,1024]{2,1,0:T(8,128)(2,1)S(1)}, u32[]{:S(2)}, u32[]{:S(2)}) collective-permute-start(bf16[2,32,1024]{2,1,0:T(8,128)(2,1)S(1)} %get-tuple-element.28), channel_id=1, source_target_pairs={{0,32},{16,48},{32,0},{48,16},{1,33},{17,49},{33,1},{49,17},{2,34}... | collective-permute-start | bytes 393224 | tf_op jit(solution)/shard_map/ppermute | solution.py:23
  43.7 6.5 %collective-permute-start.13 = (bf16[4,32,1024]{2,1,0:T(8,128)(2,1)S(1)}, bf16[4,32,1024]{2,1,0:T(8,128)(2,1)S(1)}, u32[]{:S(2)}, u32[]{:S(2)}) collective-permute-start(bf16[4,32,1024]{2,1,0:T(8,128)(2,1)S(1)} %get-tuple-element.40), channel_id=1, source_target_pairs={{0,64},{64,128},{128,192},{192,0},{1,65},{65,129},{129,193},{193,1... | collective-permute-start | bytes 786440 | tf_op jit(solution)/shard_map/ppermute | solution.py:23
  44.0 14.1 %collective-permute-start.14 = (bf16[4,32,1024]{2,1,0:T(8,128)(2,1)}, bf16[4,32,1024]{2,1,0:T(8,128)(2,1)S(1)}, u32[]{:S(2)}, u32[]{:S(2)}) collective-permute-start(bf16[4,32,1024]{2,1,0:T(8,128)(2,1)} %get-tuple-element.38), channel_id=1, source_target_pairs={{0,192},{64,0},{128,64},{192,128},{1,193},{65,1},{129,65},{193,129... | collective-permute-start | bytes 786440 | tf_op jit(solution)/shard_map/ppermute | solution.py:23
  46.3 14.6 %collective-permute-start.15 = (bf16[4,32,1024]{2,1,0:T(8,128)(2,1)S(1)}, bf16[4,32,1024]{2,1,0:T(8,128)(2,1)S(1)}, u32[]{:S(2)}, u32[]{:S(2)}) collective-permute-start(bf16[4,32,1024]{2,1,0:T(8,128)(2,1)S(1)} %get-tuple-element.37), channel_id=1, source_target_pairs={{0,128},{64,192},{128,0},{192,64},{1,129},{65,193},{129,1},{193,65... | collective-permute-start | bytes 786440 | tf_op jit(solution)/shard_map/ppermute | solution.py:23
  46.6 14.4 %collective-permute-start.10 = (bf16[4,32,1024]{2,1,0:T(8,128)(2,1)S(1)}, bf16[4,32,1024]{2,1,0:T(8,128)(2,1)S(1)}, u32[]{:S(2)}, u32[]{:S(2)}) collective-permute-start(bf16[4,32,1024]{2,1,0:T(8,128)(2,1)S(1)} %pad_maximum_fusion.3.refs_0_), channel_id=1, source_target_pairs={{0,16},{16,32},{32,48},{48,0},{1,17},{17,33},{33,49},{49,1},{2,18}... | collective-permute-start | bytes 786440 | tf_op jit(solution)/shard_map/ppermute | solution.py:23
  46.9 14.1 %collective-permute-start.11 = (bf16[4,32,1024]{2,1,0:T(8,128)(2,1)S(1)}, bf16[4,32,1024]{2,1,0:T(8,128)(2,1)S(1)}, u32[]{:S(2)}, u32[]{:S(2)}) collective-permute-start(bf16[4,32,1024]{2,1,0:T(8,128)(2,1)S(1)} %pad_maximum_fusion.3.refs_0_), channel_id=1, source_target_pairs={{0,48},{16,0},{32,16},{48,32},{1,49},{17,1},{33,17},{49,33},{2,50}... | collective-permute-start | bytes 786440 | tf_op jit(solution)/shard_map/ppermute | solution.py:23
  50.1 16.8 %collective-permute-start.12 = (bf16[4,32,1024]{2,1,0:T(8,128)(2,1)S(1)}, bf16[4,32,1024]{2,1,0:T(8,128)(2,1)S(1)}, u32[]{:S(2)}, u32[]{:S(2)}) collective-permute-start(bf16[4,32,1024]{2,1,0:T(8,128)(2,1)S(1)} %pad_maximum_fusion.3.refs_0_), channel_id=1, source_target_pairs={{0,32},{16,48},{32,0},{48,16},{1,33},{17,49},{33,1},{49,17},{2,34}... | collective-permute-start | bytes 786440 | tf_op jit(solution)/shard_map/ppermute | solution.py:23
  69.4 23.6 %collective-permute-start.16 = (bf16[16,2,32,256]{3,2,1,0:T(8,128)(2,1)S(1)}, bf16[16,2,32,256]{3,2,1,0:T(8,128)(2,1)S(1)}, u32[]{:S(2)}, u32[]{:S(2)}) collective-permute-start(bf16[16,2,32,256]{3,2,1,0:T(8,128)(2,1)S(1)} %get-tuple-element.24), channel_id=1, source_target_pairs={{0,0},{1,64},{64,1},{65,65},{128,128},{129,192},{192,129},{193,193... | collective-permute-start | bytes 1572872 | tf_op jit(solution)/shard_map/ppermute | solution.py:217
  75.2 20.6 %collective-permute-start.17 = (bf16[16,2,32,256]{3,2,1,0:T(8,128)(2,1)S(1)}, bf16[16,2,32,256]{3,2,1,0:T(8,128)(2,1)S(1)}, u32[]{:S(2)}, u32[]{:S(2)}) collective-permute-start(bf16[16,2,32,256]{3,2,1,0:T(8,128)(2,1)S(1)} %get-tuple-element.23), channel_id=1, source_target_pairs={{0,64},{1,0},{64,65},{65,1},{128,192},{129,128},{192,193},{193,129... | collective-permute-start | bytes 1572872 | tf_op jit(solution)/shard_map/ppermute | solution.py:217
  178.3 20.1 %all-to-all-start.2 = ((bf16[16,128,256]{2,1,0:T(8,128)(2,1)}), bf16[16,128,256]{2,1,0:T(8,128)(2,1)S(1)}, u32[]{:S(2)}, u32[]{:S(2)}) async-start(bf16[16,128,256]{2,1,0:T(8,128)(2,1)} %bitcast.37), calls=%async_computation.2 | async-start | bytes 2097152 | tf_op jit(solution)/shard_map/all_to_all | solution.py:234
Sparse Core Ops, SparseCore 0:
  30.2 93.0 all-gather.2
  125.7 59.1 all-gather.4
